TPU v7x, 256 devices: a whole 4x4x8 slice. The times are simulated.
256 devices in a mesh: vol: 32 (over x, z), view: 8 (over y, core).
Axes of the slice: x: 4, y: 4, z: 8, core: 2. Of those that a mesh axis runs over, the one named last changes fastest.
Arguments:
- volume: float32 [16, 32768], P(None, 'vol'), may hold values from -6 to 6
- row_footprint: float32 [64, 32, 80, 16], P('view', 'vol'), may hold values from 0 to 2.4, as said below
- column_footprint_weights: bfloat16 [32768, 3072], P('vol'), may hold values from 0 to 0.5, as said below
- tile_rows: int32 [32], P('vol'), may hold values from 0 to 16
- table_offset: int32 [64], P('view'), may hold values from 0 to 31
- view_angle: int32 [64], P('view'), may hold values from 0 to 3071
- measured: float32 [128, 64, 3072], P('vol', 'view'), may hold values from -6 to 6
- row_scale: float32 [128, 64, 3072], P('vol', 'view'), may hold values from 0.1 to 1
- column_scale: float32 [16, 32768], P(None, 'vol'), may hold values from 0.01 to 0.1
Outputs:
- updated: float32 [16, 32768], P(None, 'vol')
- weighted: float32 [128, 64, 3072], P('vol', 'view')
Inputs may be any that keep to these rules, and one draw needn't show every extreme that they name: `row_footprint`: nonnegative banded weights. `column_footprint_weights`: nonnegative banded weights.
All inputs are finite; a program needn't handle non-finite values.
Results may differ from a plain program's by a relative error of at most 0.0026.
Values may be sent and summed in bfloat16 or wider, within the bound.
A program may use at most 128 MiB of HBM per device.

v0:
```python
import jax
import jax.numpy as jnp
from jax import lax
from jax.sharding import PartitionSpec as P


def selector(row_count, starts, foot_rows, dtype):
    row_ids = lax.broadcasted_iota(jnp.int32, (starts.shape[0], row_count, foot_rows), 1)
    foot_ids = lax.broadcasted_iota(jnp.int32, (starts.shape[0], row_count, foot_rows), 2)
    return (row_ids - starts[:, None, None] == foot_ids).astype(dtype)


def body(
    volume,
    row_footprint,
    column_footprint_weights,
    tile_rows,
    table_offset,
    view_angle,
    measured,
    row_scale,
    column_scale,
):
    own_rows = measured.shape[0]
    owning_devices = lax.axis_size("vol")
    all_rows = own_rows * owning_devices
    footprint = row_footprint[:, 0]
    foot_rows = footprint.shape[1]
    starts = tile_rows[0] + table_offset
    forward_projected = jnp.einsum(
        "vfs,sk->vfk", footprint, volume, precision=lax.Precision.HIGHEST
    ).astype(jnp.bfloat16)
    block_list = jnp.einsum(
        "xot,tb->xob",
        forward_projected,
        column_footprint_weights,
        preferred_element_type=jnp.float32,
    )
    block_list = jax.vmap(lambda block_data, shift_cols: jnp.roll(block_data, shift_cols, axis=1))(
        block_list, view_angle
    )
    placement_matrix = selector(own_rows * lax.axis_size("vol"), starts, foot_rows, jnp.float32)
    projection = lax.psum_scatter(
        jnp.einsum("eba,eaq->beq", placement_matrix, block_list, precision=lax.Precision.HIGHEST),
        "vol",
        scatter_dimension=0,
        tiled=True,
    )
    weighted = row_scale * (measured - projection)
    sent_rows = weighted.astype(jnp.bfloat16)
    collected_rows = lax.all_gather(sent_rows, "vol", axis=0, tiled=True)
    selection_matrix = jnp.swapaxes(selector(all_rows, starts, foot_rows, jnp.bfloat16), 1, 2)
    detector_windows = jnp.einsum(
        "enl,leg->eng", selection_matrix, collected_rows, preferred_element_type=jnp.float32
    ).astype(jnp.bfloat16)
    detector_windows = jax.vmap(lambda window, shift_cols: jnp.roll(window, -shift_cols, axis=1))(
        detector_windows, view_angle
    )
    back_cols = jnp.einsum(
        "bgn,an->bga",
        detector_windows,
        column_footprint_weights,
        preferred_element_type=jnp.float32,
    )
    back_sum = jnp.einsum("vfs,vfk->sk", footprint, back_cols, precision=lax.Precision.HIGHEST)
    total_update = lax.psum(back_sum, "view")
    updated = volume + column_scale * total_update
    return (updated, weighted)


def solution(mesh):
    placed = (
        P(None, "vol"),
        P("view", "vol", None, None),
        P("vol", None),
        P("vol"),
        P("view"),
        P("view"),
        P("vol", "view", None),
        P("vol", "view", None),
        P(None, "vol"),
    )
    return jax.shard_map(
        body,
        mesh=mesh,
        in_specs=placed,
        out_specs=(P(None, "vol"), P("vol", "view", None)),
        check_vma=False,
    )
```

profile of v0, /device:TPU:1, one launch (start us, length us, event | category | flops | bytes accessed | tf_op | source)
XLA Modules:
  0.0 548.1 jit_solution(11968481994840157446)
XLA Ops:
  8.0 3.1 convolution_convert_fusion
  11.1 6.3 %fusion.2 = f32[8,80,3072]{2,1,0:T(8,128)S(1)} fusion(bf16[8,80,1024]{2,1,0:T(8,128)(2,1)S(1)} %convolution_convert_fusion, bf16[1024,3072]{1,0:T(8,128)(2,1)} %param.11), kind=kOutput, calls=%fused_computation.9 | convolution fusion | flops 4026531840 | bytes 15466496 | tf_op jit(solution)/shard_map/xot,tb->xob/dot_general | solution.py:33
  17.4 5.8 %pad_maximum_fusion = f32[8,80,6144]{2,1,0:T(8,128)} fusion(f32[8,80,3072]{2,1,0:T(8,128)S(1)} %fusion.2), kind=kLoop, calls=%fused_computation.4 | loop fusion | flops 3932160 | bytes 23592960 | tf_op jit(solution)/shard_map/vmap(jit(_roll_dynamic))/concatenate | solution.py:39
  23.2 36.0 %while.2 = (s32[]{:T(128)}, f32[8,80,6144]{2,1,0:T(8,128)}, s32[8,3]{0,1:T(4,128)S(1)}, f32[8,80,3072]{2,1,0:T(8,128)}, s32[]{:T(128)}) while((s32[]{:T(128)}, f32[8,80,6144]{2,1,0:T(8,128)}, s32[8,3]{0,1:T(4,128)S(1)}, f32[8,80,3072]{2,1,0:T(8,128)}, s32[]{:T(128)}) %tuple.41), condition=%wide.while_cond, body=%wide.while_body.sunk | while | flops 2 | bytes 1967721 | solution.py:39
  23.9 3.8 dynamic-slice_dynamic-update-slice_fusion.4
  28.4 3.8 dynamic-slice_dynamic-update-slice_fusion.4
  32.9 3.9 dynamic-slice_dynamic-update-slice_fusion.4
  37.4 3.8 dynamic-slice_dynamic-update-slice_fusion.4
  41.9 3.8 dynamic-slice_dynamic-update-slice_fusion.4
  46.4 3.8 dynamic-slice_dynamic-update-slice_fusion.4
  50.9 3.8 dynamic-slice_dynamic-update-slice_fusion.4
  55.4 3.8 dynamic-slice_dynamic-update-slice_fusion.4
  59.9 15.0 %convolution_bitcast_fusion = f32[128,8,3072]{0,2,1:T(8,128)} fusion(f32[8,80,3072]{2,1,0:T(8,128)} %get-tuple-element.9, s32[8]{0:T(128)S(1)} %broadcast_add_fusion), kind=kOutput, calls=%fused_computation.6 | convolution fusion | flops 3020062720 | bytes 20447264 | tf_op jit(solution)/shard_map/eba,eaq->beq/dot_general | solution.py:44
  74.9 12.9 %copy.14 = f32[128,8,3072]{2,1,0:T(8,128)} copy(f32[128,8,3072]{0,2,1:T(8,128)} %convolution_bitcast_fusion) | data formatting | bytes 25165824 | tf_op jit(solution)/shard_map/eba,eaq->beq/transpose | solution.py:44
  87.9 238.0 %reduce-scatter.2.cloned.1.call-done = f32[4,8,3072]{2,1,0:T(8,128)} async-done(((f32[128,8,3072]{2,1,0:T(8,128)}), f32[4,8,3072]{2,1,0:T(8,128)}) %reduce-scatter.2.cloned.1.call-update) | async-done | bytes 393232 | tf_op jit(solution)/shard_map/reduce_scatter | solution.py:43
  325.9 1.9 fusion.16
  328.0 91.3 %all-gather.2.cloned.1.call-done = bf16[128,8,3072]{2,1,0:T(8,128)(2,1)} async-done(((bf16[4,8,3072]{2,1,0:T(8,128)(2,1)}), bf16[128,8,3072]{2,1,0:T(8,128)(2,1)}) %all-gather.2.cloned.1.call-update) | async-done | bytes 6291472 | tf_op jit(solution)/shard_map/all_gather | solution.py:51
  419.4 12.2 %fusion.6 = bf16[8,80,3072]{2,1,0:T(8,128)(2,1)} fusion(bf16[128,8,3072]{2,1,0:T(8,128)(2,1)} %all-gather.2.cloned.1.call-done, s32[8]{0:T(128)S(1)} %broadcast_add_fusion), kind=kOutput, calls=%fused_computation.13 | convolution fusion | flops 505446400 | bytes 10223648 | tf_op jit(solution)/shard_map/enl,leg->eng/dot_general | solution.py:53
  431.6 7.3 %pad_maximum_fusion.1 = bf16[8,80,6144]{2,1,0:T(8,128)(2,1)} fusion(bf16[8,80,3072]{2,1,0:T(8,128)(2,1)} %fusion.6), kind=kLoop, calls=%fused_computation.5 | loop fusion | flops 15728640 | bytes 11796480 | tf_op jit(solution)/shard_map/vmap(jit(_roll_dynamic))/concatenate | solution.py:56
  438.9 32.2 %while.3 = (s32[]{:T(128)}, bf16[8,80,6144]{2,1,0:T(8,128)(2,1)}, s32[8,3]{0,1:T(4,128)S(1)}, bf16[8,80,3072]{2,1,0:T(8,128)(2,1)}, s32[]{:T(128)}) while((s32[]{:T(128)}, bf16[8,80,6144]{2,1,0:T(8,128)(2,1)}, s32[8,3]{0,1:T(4,128)S(1)}, bf16[8,80,3072]{2,1,0:T(8,128)(2,1)}, s32[]{:T(128)}) %tuple.44), condition=%wide.while_cond.1, body=%wide.while_body.1.sunk | while | flops 2 | bytes 984681 | solution.py:56
  439.5 3.4 dynamic-slice_dynamic-update-slice_fusion.5
  443.6 3.4 dynamic-slice_dynamic-update-slice_fusion.5
  447.6 3.4 dynamic-slice_dynamic-update-slice_fusion.5
  451.7 3.3 dynamic-slice_dynamic-update-slice_fusion.5
  455.7 3.3 dynamic-slice_dynamic-update-slice_fusion.5
  459.7 3.4 dynamic-slice_dynamic-update-slice_fusion.5
  463.7 3.4 dynamic-slice_dynamic-update-slice_fusion.5
  467.8 3.3 dynamic-slice_dynamic-update-slice_fusion.5
  471.1 7.6 %fusion = f32[8,80,1024]{2,1,0:T(8,128)S(1)} fusion(bf16[8,80,3072]{2,1,0:T(8,128)(2,1)} %get-tuple-element.17, bf16[1024,3072]{1,0:T(8,128)(2,1)} %param.11), kind=kOutput, calls=%fused_computation.7 | convolution fusion | flops 4026531840 | bytes 12845056 | tf_op jit(solution)/shard_map/bgn,an->bga/dot_general | solution.py:59
  478.7 2.1 convolution_bitcast_fusion.1
  480.8 59.3 %all-reduce.4.cloned.1.call-done = f32[16,1024]{1,0:T(8,128)} async-done(((f32[16,1024]{1,0:T(8,128)}), f32[16,1024]{1,0:T(8,128)}) %all-reduce.4.cloned.1.call-update) | async-done | bytes 65552 | tf_op jit(solution)/shard_map/psum | solution.py:66
  540.1 1.5 multiply_add_fusion
  (56 shorter events, 11.9 us)
Async XLA Ops:
  7.2 0.8 copy-start
  7.2 318.7 %reduce-scatter.2.cloned.1.call-start = ((), (), s32[]{:S(2)}) async-start(), calls=%async_computation.1 | async-start | bytes 12976128 | tf_op jit(solution)/shard_map/reduce_scatter | solution.py:43
  23.2 36.7 %copy-start.5 = (s32[8]{0:T(128)S(1)}, s32[8]{0:T(128)}, u32[]{:S(2)}) copy-start(s32[8]{0:T(128)} %param.13) | copy-start | bytes 100
  87.8 238.1 %copy-start.1 = (f32[4,8,3072]{2,1,0:T(8,128)S(1)}, f32[4,8,3072]{2,1,0:T(8,128)}, u32[]{:S(2)}) copy-start(f32[4,8,3072]{2,1,0:T(8,128)} %param.16) | copy-start | bytes 1179652
  87.8 238.1 %copy-start.2 = (f32[4,8,3072]{2,1,0:T(8,128)S(1)}, f32[4,8,3072]{2,1,0:T(8,128)}, u32[]{:S(2)}) copy-start(f32[4,8,3072]{2,1,0:T(8,128)} %param.15) | copy-start | bytes 1179652
  87.8 331.5 %all-gather.2.cloned.1.call-start = ((), (), s32[]{:S(2)}) async-start(), calls=%async_computation.2 | async-start | bytes 6488064 | tf_op jit(solution)/shard_map/all_gather | solution.py:51
  327.8 212.3 %all-reduce.4.cloned.1.call-start = ((), (), s32[]{:S(2)}) async-start(), calls=%async_computation.3 | async-start | bytes 131072 | tf_op jit(solution)/shard_map/psum | solution.py:66
  471.1 69.0 %copy-start.3 = (f32[16,1024]{1,0:T(8,128)S(1)}, f32[16,1024]{1,0:T(8,128)}, u32[]{:S(2)}) copy-start(f32[16,1024]{1,0:T(8,128)} %param.9) | copy-start | bytes 196612
  471.1 69.0 %copy-start.4 = (f32[16,1024]{1,0:T(8,128)S(1)}, f32[16,1024]{1,0:T(8,128)}, u32[]{:S(2)}) copy-start(f32[16,1024]{1,0:T(8,128)} %param.17) | copy-start | bytes 196612
Sparse Core Ops, SparseCore 0:
  88.0 237.9 reduce-scatter.1
  328.5 90.8 all-gather.1
  481.0 59.1 all-reduce.3
where the time goes:
time: 551 us; the launch traced here: 548 us
  waiting for transfers between devices  389 us (71%)
  local copies, waits for them, and re-layouts  81.2 us (15%)
  matrix products  46.3 us (8%)
  other arithmetic  17.1 us (3%)
  between operations  14.5 us (3%)
    reduce_scatter x1, waiting for transfers between devices, body(): lax.psum_scatter(jnp.einsum('eba,eaq->beq', placement_matrix, block_list,...  238 us
    all_gather x1, waiting for transfers between devices, body(): collected_rows = lax.all_gather(sent_rows, 'vol', axis=0, tiled=True)  91.3 us
    gather x48, local copies, waits for them, and re-layouts  68.2 us
    psum x1, waiting for transfers between devices, body(): total_update = lax.psum(back_sum, 'view')  59.3 us
    dot_general x1, matrix products, body(): jnp.einsum('eba,eaq->beq', placement_matrix, block_list, precision=lax.Pr...  15 us
    transpose x1, local copies, waits for them, and re-layouts, body(): jnp.einsum('eba,eaq->beq', placement_matrix, block_list, precision=lax.Pr...  12.9 us
    dot_general x1, matrix products, body(): jnp.einsum('enl,leg->eng', selection_matrix, collected_rows, preferred_el...  12.2 us
  transfers between devices with their start and end apart: 3, of which 3 were waited for; matrix products, arithmetic and copies ran while one was open for 0% of the time, Pallas kernels for 0%

commit v1 on v0

v1 whole, which is shorter than its diff:
```python
import functools

import jax
import jax.numpy as jnp
from jax import lax
from jax.experimental import pallas as pl
from jax.experimental.pallas import tpu as pltpu
from jax.sharding import PartitionSpec as P

MESH = pl.DeviceIdType.MESH
F32, BF16 = jnp.float32, jnp.bfloat16
S, FR, DR, DC, KV = 16, 80, 128, 3072, 1024
NX, NY, NZ, NV = 4, 4, 8, 8
CW = DC // 8
N_COPIES = 96


def split2(a):
    hi = a.astype(BF16)
    return hi, (a - hi.astype(F32)).astype(BF16)


def barrel(a, shift):
    for bit in range(12):
        moved = pltpu.roll(a, 1 << bit, 1)
        on = jnp.broadcast_to((shift >> bit) & 1, a.shape)
        a = jnp.where(on == 1, moved, a)
    return a


def kernel(
    vol_ref, foot_ref, key_ref, ang_ref, cs_ref, c_hbm, m_hbm, r_hbm,
    upd_ref, wtd_hbm,
    cbuf, mraw, rraw, ybuf, pbuf, gbuf, gt, a4, acat, atb,
    msend, rsend, mrecv, rrecv, wsend, wrecv, wout,
    zsend, zrecv, ssend, srecv, ubuf, ucore, uy, ufin, uother,
    lsem, ssem, rsem,
):
    d = lax.axis_index("vol")
    g = lax.axis_index("view")
    x, z = d // NZ, d % NZ
    y, c = g // 2, g % 2

    def xp(o):
        return (lax.rem(x + o, NX) * NZ + z, g)

    def zp(o):
        return (x * NZ + lax.rem(z + o, NZ), g)

    def vp(o):
        return (d, lax.rem(g + o, NV))

    def yp(o):
        return (d, lax.rem(y + o, NY) * 2 + c)

    core = (d, y * 2 + (1 - c))

    counter = [0]
    started = []

    def send(src, dst, device):
        n = counter[0]
        counter[0] += 1
        copy = pltpu.make_async_remote_copy(
            src_ref=src, dst_ref=dst, send_sem=ssem.at[n], recv_sem=rsem.at[n],
            device_id=device, device_id_type=MESH,
        )
        copy.start()
        started.append(copy)
        return copy

    barrier = pltpu.get_barrier_semaphore()
    partners = [xp(o) for o in range(1, NX)] + [zp(o) for o in range(1, NZ)] + [vp(o) for o in range(1, NV)]
    for device in partners:
        pl.semaphore_signal(barrier, inc=1, device_id=device, device_id_type=MESH)

    col0 = pl.multiple_of(g * CW, 128)
    c_in = pltpu.make_async_copy(c_hbm.at[:, pl.ds(col0, CW)], cbuf, lsem.at[0])
    m_in = pltpu.make_async_copy(m_hbm, mraw, lsem.at[1])
    r_in = pltpu.make_async_copy(r_hbm, rraw, lsem.at[2])
    c_in.start()
    m_in.start()
    r_in.start()

    f_hi, f_rest = split2(foot_ref[...])
    f_mid, f_lo = split2(foot_ref[...] - f_hi.astype(F32))
    f_all = jnp.concatenate([f_hi, f_mid, f_lo], axis=0)
    for zz in range(NZ):
        lane = lax.broadcasted_iota(jnp.int32, (128, 8 * FR), 0)
        row = (lane // 32) * 32 + zz * 4 + (lane % 32) // 8
        one_hot = (key_ref[...] == (lane % 8) * 1024 + row).astype(F32).astype(BF16)
        placed = lax.dot_general(f_all, one_hot, (((1,), (1,)), ((), ())), preferred_element_type=F32)
        pbuf[zz] = placed[:S] + placed[S : 2 * S] + placed[2 * S :]

    v_hi, v_lo = split2(vol_ref[...])
    c_in.wait()
    prod = jnp.dot(jnp.concatenate([v_hi, v_lo], axis=0), cbuf[...], preferred_element_type=F32)
    ybuf[d] = (prod[:S] + prod[S:]).astype(BF16)

    pl.semaphore_wait(barrier, len(partners))

    y_z = [send(ybuf.at[d], ybuf.at[d], zp(o)) for o in range(1, NZ)]
    f_z = [send(pbuf.at[lax.rem(z + o, NZ)], gbuf.at[z], zp(o)) for o in range(1, NZ)]
    y_x = [send(ybuf.at[d], ybuf.at[d], xp(o)) for o in range(1, NX)]
    gbuf[z] = pbuf[z]

    shift_back = jnp.where(ang_ref[...] == 0, 0, DC - ang_ref[...])
    exchanged = []
    for copy_in, raw, out, got in ((m_in, mraw, msend, mrecv), (r_in, rraw, rsend, rrecv)):
        copy_in.wait()
        for i in range(4):
            rolled = barrel(raw[8 * i : 8 * i + 8, :], shift_back)
            for k in range(NV):
                out[k, 8 * i : 8 * i + 8, :] = rolled[:, k * CW : (k + 1) * CW]
        for o in range(1, NV):
            exchanged.append(send(out.at[lax.rem(g + o, NV)], got.at[g], vp(o)))
        got[g] = out[g]

    for copy in f_z:
        copy.wait_recv()
    turned = jnp.transpose(gbuf[...].reshape(NZ * S, 128))
    gt[...] = turned.reshape(NX, 32, 128)
    f_x = [send(gt.at[lax.rem(x + o, NX)], a4.at[g, x], xp(o)) for o in range(1, NX)]
    a4[g, x] = gt[x]

    for o in range(1, NZ):
        y_z[o - 1].wait_recv()
        tile = x * NZ + lax.rem(z + NZ - o, NZ)
        y_x += [send(ybuf.at[tile], ybuf.at[tile], xp(p)) for p in range(1, NX)]

    for copy in f_x:
        copy.wait_recv()
    f_c = [send(a4.at[g], a4.at[g], core)]
    f_y = [send(a4.at[g], a4.at[g], yp(o)) for o in range(1, NY)]
    for o in range(1, NY):
        f_y[o - 1].wait_recv()
        group = lax.rem(y + NY - o, NY) * 2 + c
        f_c.append(send(a4.at[group], a4.at[group], core))
    for copy in f_c:
        copy.wait_recv()

    for k in range(NX):
        part = a4[:, k].reshape(NV * 32, 128)
        hi, lo = split2(part)
        acat[0:256, k * 128 : (k + 1) * 128] = hi
        acat[256:512, k * 128 : (k + 1) * 128] = lo
        t_hi, t_lo = split2(jnp.transpose(part))
        atb[k, :, 0:256] = t_hi
        atb[k, :, 256:512] = t_lo

    for copy in y_x:
        copy.wait_recv()
    proj = jnp.dot(acat[...], ybuf[...].reshape(NX * NZ * S, CW), preferred_element_type=F32)
    proj = proj[:256] + proj[256:]
    for copy in exchanged:
        copy.wait_recv()
    weighted = rrecv[...].reshape(256, CW) * (mrecv[...].reshape(256, CW) - proj)
    wsend[...] = weighted.reshape(NV, 32, CW)
    w_bf = weighted.astype(BF16)
    w_two = jnp.concatenate([w_bf, w_bf], axis=0)
    z_x = []
    for o in (1, 2, 3, 0):
        k = lax.rem(x + o, NX)
        part = jnp.dot(atb[k], w_two, preferred_element_type=F32)
        zsend[o] = part.astype(BF16)
        if o:
            z_x.append(send(zsend.at[o], zrecv.at[o - 1], xp(o)))

    w_v = [send(wsend.at[lax.rem(g + o, NV)], wrecv.at[g], vp(o)) for o in range(1, NV)]
    wrecv[g] = wsend[g]

    for copy in z_x:
        copy.wait_recv()
    total = zsend[0].astype(F32)
    for o in range(NX - 1):
        total += zrecv[o].astype(F32)
    ssend[...] = total.astype(BF16).reshape(NZ, S, CW)
    s_z = [send(ssend.at[lax.rem(z + o, NZ)], srecv.at[o - 1], zp(o)) for o in range(1, NZ)]

    for copy in w_v:
        copy.wait_recv()
    for i in range(4):
        row = jnp.concatenate([wrecv[k, 8 * i : 8 * i + 8, :] for k in range(NV)], axis=1)
        wout[8 * i : 8 * i + 8, :] = barrel(row, ang_ref[...])
    w_out = pltpu.make_async_copy(wout, wtd_hbm, lsem.at[3])
    w_out.start()

    for copy in s_z:
        copy.wait_recv()
    total = ssend[z].astype(F32)
    for o in range(NZ - 1):
        total += srecv[o].astype(F32)
    s_hi, s_lo = split2(total)
    back = lax.dot_general(
        jnp.concatenate([s_hi, s_lo], axis=0), cbuf[...], (((1,), (1,)), ((), ())), preferred_element_type=F32
    )
    back = back[:S] + back[S:]
    ubuf[0] = back[:, : KV // 2]
    ubuf[1] = back[:, KV // 2 :]
    u_c = send(ubuf.at[1 - c], ucore, core)
    u_c.wait_recv()
    uy[y] = ubuf[c] + ucore[...]
    u_y = [send(uy.at[y], uy.at[y], yp(o)) for o in range(1, NY)]
    for copy in u_y:
        copy.wait_recv()
    total = ((uy[0] + uy[1]) + uy[2]) + uy[3]
    half = pl.ds(pl.multiple_of(c * (KV // 2), 128), KV // 2)
    other = pl.ds(pl.multiple_of((1 - c) * (KV // 2), 128), KV // 2)
    ufin[...] = vol_ref[:, half] + cs_ref[:, half] * total
    u_f = send(ufin, uother, core)
    upd_ref[:, half] = ufin[...]
    u_f.wait_recv()
    upd_ref[:, other] = uother[...]
    for copy in started:
        copy.wait_send()
    w_out.wait()


def body(volume, row_footprint, column_footprint_weights, tile_rows, table_offset, view_angle, measured, row_scale, column_scale):
    starts = tile_rows[0] + table_offset
    key = (jnp.arange(8, dtype=jnp.int32)[:, None] * 1024 + starts[:, None] + jnp.arange(FR, dtype=jnp.int32)[None, :]).reshape(1, 8 * FR)
    foot = row_footprint[:, 0].reshape(8 * FR, S).T
    vmem = pl.BlockSpec(memory_space=pltpu.VMEM)
    hbm = pl.BlockSpec(memory_space=pl.ANY)
    updated, weighted = pl.pallas_call(
        kernel,
        out_shape=(jax.ShapeDtypeStruct((S, KV), F32), jax.ShapeDtypeStruct((32, DC), F32)),
        in_specs=[vmem] * 5 + [hbm] * 3,
        out_specs=(vmem, hbm),
        scratch_shapes=[
            pltpu.VMEM((KV, CW), BF16),
            pltpu.VMEM((32, DC), F32),
            pltpu.VMEM((32, DC), F32),
            pltpu.VMEM((32, S, CW), BF16),
            pltpu.VMEM((NZ, S, 128), F32),
            pltpu.VMEM((NZ, S, 128), F32),
            pltpu.VMEM((NX, 32, 128), F32),
            pltpu.VMEM((NV, NX, 32, 128), F32),
            pltpu.VMEM((512, 512), BF16),
            pltpu.VMEM((NX, 128, 512), BF16),
            pltpu.VMEM((NV, 32, CW), F32),
            pltpu.VMEM((NV, 32, CW), F32),
            pltpu.VMEM((NV, 32, CW), F32),
            pltpu.VMEM((NV, 32, CW), F32),
            pltpu.VMEM((NV, 32, CW), F32),
            pltpu.VMEM((NV, 32, CW), F32),
            pltpu.VMEM((32, DC), F32),
            pltpu.VMEM((NX, 128, CW), BF16),
            pltpu.VMEM((NX - 1, 128, CW), BF16),
            pltpu.VMEM((NZ, S, CW), BF16),
            pltpu.VMEM((NZ - 1, S, CW), BF16),
            pltpu.VMEM((2, S, KV // 2), F32),
            pltpu.VMEM((S, KV // 2), F32),
            pltpu.VMEM((NY, S, KV // 2), F32),
            pltpu.VMEM((S, KV // 2), F32),
            pltpu.VMEM((S, KV // 2), F32),
            pltpu.SemaphoreType.DMA((4,)),
            pltpu.SemaphoreType.DMA((N_COPIES,)),
            pltpu.SemaphoreType.DMA((N_COPIES,)),
        ],
        compiler_params=pltpu.CompilerParams(collective_id=0, has_side_effects=True, vmem_limit_bytes=40 << 20),
        cost_estimate=pl.CostEstimate(flops=500_000_000, bytes_accessed=3_000_000, transcendentals=0),
        name="sirt",
    )(
        volume, foot, key, view_angle.reshape(8, 1), column_scale, column_footprint_weights,
        measured.reshape(32, DC), row_scale.reshape(32, DC),
    )
    return updated, weighted.reshape(4, 8, DC)


def solution(mesh):
    placed = (
        P(None, "vol"),
        P("view", "vol", None, None),
        P("vol", None),
        P("vol"),
        P("view"),
        P("view"),
        P("vol", "view", None),
        P("vol", "view", None),
        P(None, "vol"),
    )
    return jax.shard_map(
        body,
        mesh=mesh,
        in_specs=placed,
        out_specs=(P(None, "vol"), P("vol", "view", None)),
        check_vma=False,
    )
```

time: 551 us -> 59.6 us (0.11)
  waiting for transfers between devices: 389 us -> 0 us
  local copies, waits for them, and re-layouts: 81.2 us -> 9.59 us
  Pallas kernels: 0 us -> 47.6 us
  matrix products: 46.3 us -> 0 us
  other arithmetic: 17.1 us -> 0.73 us
  between operations: 14.5 us -> 1.31 us
    reduce_scatter x1 -> x0, waiting for transfers between devices: 238 us -> none  [body(): lax.psum_scatter(jnp.einsum('eba,eaq->beq', placement_matrix, block_list,...]
    all_gather x1 -> x0, waiting for transfers between devices: 91.3 us -> none  [body(): collected_rows = lax.all_gather(sent_rows, 'vol', axis=0, tiled=True)]
    gather x48 -> x0, local copies, waits for them, and re-layouts: 68.2 us -> none
    psum x1 -> x0, waiting for transfers between devices: 59.3 us -> none  [body(): total_update = lax.psum(back_sum, 'view')]
    pallas_call x0 -> x1, Pallas kernels: none -> 47.6 us  [body(): pl.pallas_call(kernel, out_shape=(jax.ShapeDtypeStruct((S, KV), F32), jax...]
    dot_general x6 -> x0, matrix products: 46.3 us -> none  [the longest x1 15 us: body(): jnp.einsum('eba,eaq->beq', placement_matrix, block_list, precision=lax.Pr...]
    concatenate x2 -> x0, other arithmetic: 13.1 us -> none  [the longest x1 7.28 us: body(): jnp.roll(window, -shift_cols, axis=1)]
    transpose x1 -> x0, local copies, waits for them, and re-layouts: 12.9 us -> none  [body(): jnp.einsum('eba,eaq->beq', placement_matrix, block_list, precision=lax.Pr...]
  transfers between devices with their start and end apart: 3 -> 0, of which waited for: 3 -> 0; matrix products, arithmetic and copies ran while one was open for 0% -> 0% of each run, Pallas kernels for 0% -> 0%
where the time goes in v1:
time: 59.6 us; the launch traced here: 59.2 us
  Pallas kernels  47.6 us (80%)
  local copies, waits for them, and re-layouts  9.59 us (16%)
  between operations  1.31 us (2%)
  other arithmetic  0.73 us (1%)
    pallas_call x1, Pallas kernels, body(): pl.pallas_call(kernel, out_shape=(jax.ShapeDtypeStruct((S, KV), F32), jax...  47.6 us
    unnamed x13, local copies, waits for them, and re-layouts  8.69 us

profile of v1, /device:TPU:1, one launch (start us, length us, event | category | flops | bytes accessed | tf_op | source)
XLA Modules:
  0.0 59.2 jit_solution(10743335647606297226)
XLA Ops:
  1.3 0.7 %add_add_fusion = s32[8]{0:T(128)S(1)} fusion(s32[8]{0:T(128)} %param.13, s32[]{:T(128)} %bitcast.10), kind=kLoop, calls=%fused_computation.1 | loop fusion | flops 24 | bytes 68 | tf_op jit(solution)/shard_map/add | solution.py:221
  1.9 0.1 iota_add_fusion
  2.0 0.1 add.39.key_ref
  2.1 0.7 %copy.12.ang_ref = s32[8,1]{1,0:T(8,128)S(1)} copy(s32[8,1]{0,1:T(1,128)} %bitcast.15) | data formatting | bytes 64 | tf_op jit(solution)/shard_map/reshape | solution.py:265
  2.8 0.9 %copy.11 = f32[8,1,80,16]{2,0,3,1:T(8,128)S(1)} copy(f32[8,1,80,16]{2,3,1,0:T(8,128)} %param.10) | data formatting | bytes 81920 | tf_op args[1]
  3.7 0.1 reshape_squeeze.3
  3.8 0.0 copy-start
  3.8 2.8 %copy-done = bf16[1024,3072]{1,0:T(8,128)(2,1)S(1)} copy-done((bf16[1024,3072]{1,0:T(8,128)(2,1)S(1)}, bf16[1024,3072]{1,0:T(8,128)(2,1)}, u32[]{:S(2)}) %copy-start) | copy-done | bytes 6291480
  6.6 0.0 copy-start.1
  6.6 1.0 %copy-done.1 = f32[4,8,3072]{2,1,0:T(8,128)S(1)} copy-done((f32[4,8,3072]{2,1,0:T(8,128)S(1)}, f32[4,8,3072]{2,1,0:T(8,128)}, u32[]{:S(2)}) %copy-start.1) | copy-done | bytes 393240
  7.6 0.0 copy-start.2
  7.6 1.0 %copy-done.2 = f32[4,8,3072]{2,1,0:T(8,128)S(1)} copy-done((f32[4,8,3072]{2,1,0:T(8,128)S(1)}, f32[4,8,3072]{2,1,0:T(8,128)}, u32[]{:S(2)}) %copy-start.2) | copy-done | bytes 393240
  8.6 0.0 copy-start.3
  8.6 0.8 %copy-done.3 = f32[16,1024]{1,0:T(8,128)S(1)} copy-done((f32[16,1024]{1,0:T(8,128)S(1)}, f32[16,1024]{1,0:T(8,128)}, u32[]{:S(2)}) %copy-start.3) | copy-done | bytes 65560
  9.4 0.0 copy-start.4
  9.4 0.8 %copy-done.4 = f32[16,1024]{1,0:T(8,128)S(1)} copy-done((f32[16,1024]{1,0:T(8,128)S(1)}, f32[16,1024]{1,0:T(8,128)}, u32[]{:S(2)}) %copy-start.4) | copy-done | bytes 65560
  10.2 47.6 %sirt.1 = (f32[16,1024]{1,0:T(8,128)S(1)}, f32[32,3072]{1,0:T(8,128)S(1)}) custom-call(f32[16,1024]{1,0:T(8,128)S(1)} %copy-done.3, f32[16,640]{1,0:T(8,128)S(1)} %bitcast.14, s32[1,640]{1,0:T(1,128)S(1)} %add.39.key_ref, s32[8,1]{1,0:T(8,128)S(1)} %copy.12.ang_ref, f32[16,1024]{1,0:T(8,128)S(1)} %copy-done.4, bf16[1024,3072]{1,0:T(8,128)(2,1)S(1)} %copy-done, ...), custom_call_target="tpu_custom_call" | custom-call | flops 500000000 | bytes 3000000 | tf_op jit(solution)/shard_map/sirt/pallas_call | solution.py:225
  57.9 0.6 %copy.16 = f32[16,1024]{1,0:T(8,128)} copy(f32[16,1024]{1,0:T(8,128)S(1)} %get-tuple-element.8) | data formatting | bytes 131072
  58.5 0.7 %copy.17 = f32[4,8,3072]{2,1,0:T(8,128)} copy(f32[4,8,3072]{2,1,0:T(8,128)S(1)} %bitcast.13) | data formatting | bytes 786432
Async XLA Ops:
  3.8 2.8 %copy-start = (bf16[1024,3072]{1,0:T(8,128)(2,1)S(1)}, bf16[1024,3072]{1,0:T(8,128)(2,1)}, u32[]{:S(2)}) copy-start(bf16[1024,3072]{1,0:T(8,128)(2,1)} %c_hbm.1) | copy-start | bytes 18874372
  6.6 1.0 %copy-start.1 = (f32[4,8,3072]{2,1,0:T(8,128)S(1)}, f32[4,8,3072]{2,1,0:T(8,128)}, u32[]{:S(2)}) copy-start(f32[4,8,3072]{2,1,0:T(8,128)} %param.15) | copy-start | bytes 1179652
  7.6 1.0 %copy-start.2 = (f32[4,8,3072]{2,1,0:T(8,128)S(1)}, f32[4,8,3072]{2,1,0:T(8,128)}, u32[]{:S(2)}) copy-start(f32[4,8,3072]{2,1,0:T(8,128)} %param.16) | copy-start | bytes 1179652
  8.6 0.8 %copy-start.3 = (f32[16,1024]{1,0:T(8,128)S(1)}, f32[16,1024]{1,0:T(8,128)}, u32[]{:S(2)}) copy-start(f32[16,1024]{1,0:T(8,128)} %vol_ref.1) | copy-start | bytes 196612
  9.4 0.8 %copy-start.4 = (f32[16,1024]{1,0:T(8,128)S(1)}, f32[16,1024]{1,0:T(8,128)}, u32[]{:S(2)}) copy-start(f32[16,1024]{1,0:T(8,128)} %cs_ref.1) | copy-start | bytes 196612

commit v2 on v1

v2 whole, which is shorter than its diff:
```python
import functools

import jax
import jax.numpy as jnp
from jax import lax
from jax.experimental import pallas as pl
from jax.experimental.pallas import tpu as pltpu
from jax.sharding import PartitionSpec as P

MESH = pl.DeviceIdType.MESH
F32, BF16 = jnp.float32, jnp.bfloat16
S, FR, DR, DC, KV = 16, 80, 128, 3072, 1024
NX, NY, NZ, NV = 4, 4, 8, 8
CW = DC // 8
CHUNKS = ((0, 256), (256, 128))
N_COPIES = 160


def split2(a):
    hi = a.astype(BF16)
    return hi, (a - hi.astype(F32)).astype(BF16)


def barrel(a, shift):
    for bit in range(12):
        moved = pltpu.roll(a, 1 << bit, 1)
        on = jnp.broadcast_to((shift >> bit) & 1, a.shape)
        a = jnp.where(on == 1, moved, a)
    return a


def kernel(
    vol_hbm, foot_hbm, c_hbm, tile_hbm, offset_hbm, angle_hbm, m_hbm, r_hbm, cs_hbm,
    upd_hbm, wtd_hbm,
    vol_ref, foot_ref, cs_ref, tile_s, offset_s, angle_s, cbuf, cfull, mraw, rraw, ybuf, pbuf, gbuf, gt, a4, acat, atb,
    msend, rsend, mrecv, rrecv, psend, precv, wout,
    zsend0, zsend1, zrecv0, zrecv1, ssend0, ssend1, srecv0, srecv1, sall, ufin,
    lsem, ssem, rsem,
):
    d = lax.axis_index("vol")
    g = lax.axis_index("view")
    x, z = d // NZ, d % NZ
    y, c = g // 2, g % 2

    def xp(o):
        return (lax.rem(x + o, NX) * NZ + z, g)

    def zp(o):
        return (x * NZ + lax.rem(z + o, NZ), g)

    def vp(o):
        return (d, lax.rem(g + o, NV))

    def yp(o):
        return (d, lax.rem(y + o, NY) * 2 + c)

    def xyp(p, o):
        return (lax.rem(x + p, NX) * NZ + z, lax.rem(y + o, NY) * 2 + c)

    core = (d, y * 2 + (1 - c))

    counter = [0]
    started = []

    def send(src, dst, device):
        n = counter[0]
        counter[0] += 1
        copy = pltpu.make_async_remote_copy(
            src_ref=src, dst_ref=dst, send_sem=ssem.at[n], recv_sem=rsem.at[n],
            device_id=device, device_id_type=MESH,
        )
        copy.start()
        started.append(copy)
        return copy

    barrier = pltpu.get_barrier_semaphore()
    partners = [xp(o) for o in range(1, NX)] + [zp(o) for o in range(1, NZ)] + [vp(o) for o in range(1, NV)]
    partners += [xyp(p, o) for p in range(1, NX) for o in range(1, NY)]
    for device in partners:
        pl.semaphore_signal(barrier, inc=1, device_id=device, device_id_type=MESH)

    own_cols = pl.ds(pl.multiple_of(g * CW, 128), CW)
    fetches = [
        pltpu.make_async_copy(src, dst, lsem.at[n])
        for n, (src, dst) in enumerate((
            (tile_hbm, tile_s), (offset_hbm, offset_s), (angle_hbm, angle_s), (foot_hbm, foot_ref),
            (m_hbm, mraw), (r_hbm, rraw), (c_hbm.at[:, own_cols], cbuf), (vol_hbm, vol_ref),
            (cs_hbm, cs_ref), (c_hbm, cfull),
        ))
    ]
    for copy in fetches[:-1]:
        copy.start()
    tile_in, offset_in, angle_in, foot_in, m_in, r_in, c_in, vol_in, cs_in, cfull_in = fetches

    for copy in (tile_in, offset_in, angle_in, foot_in):
        copy.wait()
    view = lax.broadcasted_iota(jnp.int32, (8, 1), 0)
    start = jnp.zeros((8, 1), jnp.int32)
    angle = jnp.zeros((8, 1), jnp.int32)
    for v in range(8):
        start = jnp.where(view == v, tile_s[0] + offset_s[v], start)
        angle = jnp.where(view == v, angle_s[v], angle)
    foot = jnp.concatenate([jnp.pad(foot_ref[v], ((0, 0), (0, 128 - FR))) for v in range(8)], axis=1)
    f_all = jnp.concatenate(split2(foot), axis=0)
    source = lax.broadcasted_iota(jnp.int32, (128, 1024), 1)
    first = jnp.concatenate([start] * 16, axis=0)
    lane = lax.broadcasted_iota(jnp.int32, (128, 1), 0)
    for zz in range(NZ):
        wanted = (lane // 32) * 32 + zz * 4 + (lane % 32) // 8 - first
        wanted = jnp.where((wanted >= 0) & (wanted < FR), wanted + (lane % 8) * 128, -1)
        one_hot = (source == wanted).astype(F32).astype(BF16)
        placed = lax.dot_general(f_all, one_hot, (((1,), (1,)), ((), ())), preferred_element_type=F32)
        pbuf[zz] = placed[:S] + placed[S:]

    pl.semaphore_wait(barrier, len(partners))

    f_z = [send(pbuf.at[lax.rem(z + o, NZ)], gbuf.at[z], zp(o)) for o in range(1, NZ)]
    gbuf[z] = pbuf[z]

    shift_back = jnp.where(angle == 0, 0, DC - angle)
    exchanged = []
    for copy_in, raw, out, got in ((m_in, mraw, msend, mrecv), (r_in, rraw, rsend, rrecv)):
        copy_in.wait()
        for i in range(0, 4, 2):
            rolled = [barrel(raw[8 * n : 8 * n + 8, :], shift_back) for n in (i, i + 1)]
            rolled = jnp.concatenate(rolled, axis=0).astype(BF16)
            for k in range(NV):
                out[k, 8 * i : 8 * i + 16, :] = rolled[:, k * CW : (k + 1) * CW]
        for o in (4, 3, 5, 2, 6, 1, 7):
            exchanged.append(send(out.at[lax.rem(g + o, NV)], got.at[g], vp(o)))
        got[g] = out[g]

    vol_in.wait()
    v_all = jnp.concatenate(split2(vol_ref[...]), axis=0)
    c_in.wait()
    prod = jnp.dot(v_all, cbuf[...], preferred_element_type=F32)
    ybuf[d] = (prod[:S] + prod[S:]).astype(BF16)
    y_z = [send(ybuf.at[d], ybuf.at[d], zp(o)) for o in range(1, NZ)]
    y_x = [send(ybuf.at[d], ybuf.at[d], xp(o)) for o in range(1, NX)]
    cfull_in.start()

    for copy in f_z:
        copy.wait_recv()
    turned = jnp.transpose(gbuf[...].reshape(NZ * S, 128))
    gt[...] = turned.reshape(NX, 32, 128)
    f_xy = {}
    for p, o in [(p, o) for p in (0, 2, 1, 3) for o in (2, 1, 3, 0) if p or o]:
        f_xy[p, o] = send(gt.at[lax.rem(x + p, NX)], a4.at[g, x], xyp(p, o))
    a4[g, x] = gt[x]
    f_c = [send(gt.at[x], a4.at[g, x], core)]

    for o in range(1, NZ):
        y_z[o - 1].wait_recv()
        tile = x * NZ + lax.rem(z + NZ - o, NZ)
        y_x += [send(ybuf.at[tile], ybuf.at[tile], xp(p)) for p in range(1, NX)]

    for (p, o), copy in f_xy.items():
        copy.wait_recv()
        piece = a4.at[lax.rem(y + NY - o, NY) * 2 + c, lax.rem(x + NX - p, NX)]
        f_c.append(send(piece, piece, core))
    for copy in f_c:
        copy.wait_recv()

    for k in range(NX):
        part = a4[:, k].reshape(NV * 32, 128)
        hi, lo = split2(part)
        acat[0:256, k * 128 : (k + 1) * 128] = hi
        acat[256:512, k * 128 : (k + 1) * 128] = lo
        atb[k * 128 : (k + 1) * 128, :] = jnp.transpose(part).astype(BF16)

    for copy in y_x:
        copy.wait_recv()
    z_x = []
    for copy in exchanged:
        copy.wait_recv()
    for j, (first, width) in enumerate(CHUNKS):
        cols = pl.ds(first, width)
        zsend, zrecv = ((zsend0, zrecv0), (zsend1, zrecv1))[j]
        proj = jnp.dot(acat[...], ybuf[:, :, cols].reshape(NX * NZ * S, width), preferred_element_type=F32)
        proj = proj[:256] + proj[256:]
        psend[:, :, cols] = proj.reshape(NV, 32, width)
        measured = mrecv[:, :, cols].astype(F32).reshape(256, width)
        weighted = rrecv[:, :, cols].astype(F32).reshape(256, width) * (measured - proj)
        part = jnp.dot(atb[...], weighted.astype(BF16), preferred_element_type=F32)
        zsend[...] = part.astype(BF16).reshape(NX, 128, width)
        z_x.append([send(zsend.at[lax.rem(x + o, NX)], zrecv.at[o - 1], xp(o)) for o in (2, 1, 3)])

    p_v = [send(psend.at[lax.rem(g + o, NV)], precv.at[g], vp(o)) for o in (1, 7, 2, 6, 3, 5, 4)]
    precv[g] = psend[g]

    s_z = []
    for j, (first, width) in enumerate(CHUNKS):
        zsend, zrecv = ((zsend0, zrecv0), (zsend1, zrecv1))[j]
        ssend, srecv = ((ssend0, srecv0), (ssend1, srecv1))[j]
        for copy in z_x[j]:
            copy.wait_recv()
        total = zsend[x].astype(F32)
        for o in range(NX - 1):
            total += zrecv[o].astype(F32)
        ssend[...] = total.astype(BF16).reshape(NZ, S, width)
        s_z.append([send(ssend.at[lax.rem(z + o, NZ)], srecv.at[o - 1], zp(o)) for o in (4, 3, 5, 2, 6, 1, 7)])

    for j, (first, width) in enumerate(CHUNKS):
        ssend, srecv = ((ssend0, srecv0), (ssend1, srecv1))[j]
        for copy in s_z[j]:
            copy.wait_recv()
        total = ssend[z].astype(F32)
        for o in range(NZ - 1):
            total += srecv[o].astype(F32)
        sall[g, :, first : first + width] = total.astype(BF16)

    s_v = {o: send(sall.at[g], sall.at[g], vp(o)) for o in (4, 3, 5, 2, 6, 1, 7)}

    for copy in p_v:
        copy.wait_recv()
    for i in range(4):
        rows = slice(8 * i, 8 * i + 8)
        row = jnp.concatenate([precv[k, rows, :] for k in range(NV)], axis=1)
        wout[rows, :] = rraw[rows, :] * (mraw[rows, :] - barrel(row, angle))
    w_out = pltpu.make_async_copy(wout, wtd_hbm, lsem.at[10])
    w_out.start()

    cfull_in.wait()
    cs_in.wait()

    for copy in s_v.values():
        copy.wait_recv()
    both = jnp.concatenate([sall[k] for k in range(NV)], axis=1)
    total = lax.dot_general(both, cfull[...], (((1,), (1,)), ((), ())), preferred_element_type=F32)

    ufin[...] = vol_ref[...] + cs_ref[...] * total
    u_out = pltpu.make_async_copy(ufin, upd_hbm, lsem.at[11])
    u_out.start()
    for copy in started:
        copy.wait_send()
    w_out.wait()
    u_out.wait()


def hand_over(upd_in, wtd_in, upd_out, wtd_out, upd_held, wtd_held, sem):
    pieces = [(upd_in, upd_held, upd_out)] + [(wtd_in.at[i], wtd_held.at[i], wtd_out.at[i]) for i in range(4)]
    arriving = [pltpu.make_async_copy(src, held, sem.at[n]) for n, (src, held, _) in enumerate(pieces)]
    leaving = [pltpu.make_async_copy(held, dst, sem.at[5 + n]) for n, (_, held, dst) in enumerate(pieces)]
    for copy in arriving:
        copy.start()
    for n in range(5):
        arriving[n].wait()
        leaving[n].start()
    for copy in leaving:
        copy.wait()


def body(volume, row_footprint, column_footprint_weights, tile_rows, table_offset, view_angle, measured, row_scale, column_scale):
    foot = jnp.transpose(row_footprint[:, 0], (0, 2, 1))
    hbm = pl.BlockSpec(memory_space=pltpu.HBM)
    updated, weighted = pl.pallas_call(
        kernel,
        out_shape=(jax.ShapeDtypeStruct((S, KV), F32), jax.ShapeDtypeStruct((32, DC), F32)),
        in_specs=[hbm] * 9,
        out_specs=(hbm, hbm),
        scratch_shapes=[
            pltpu.VMEM((S, KV), F32),
            pltpu.VMEM((8, S, FR), F32),
            pltpu.VMEM((S, KV), F32),
            pltpu.SMEM((1,), jnp.int32),
            pltpu.SMEM((8,), jnp.int32),
            pltpu.SMEM((8,), jnp.int32),
            pltpu.VMEM((KV, CW), BF16),
            pltpu.VMEM((KV, DC), BF16),
            pltpu.VMEM((32, DC), F32),
            pltpu.VMEM((32, DC), F32),
            pltpu.VMEM((32, S, CW), BF16),
            pltpu.VMEM((NZ, S, 128), F32),
            pltpu.VMEM((NZ, S, 128), F32),
            pltpu.VMEM((NX, 32, 128), F32),
            pltpu.VMEM((NV, NX, 32, 128), F32),
            pltpu.VMEM((512, 512), BF16),
            pltpu.VMEM((512, 256), BF16),
            pltpu.VMEM((NV, 32, CW), BF16),
            pltpu.VMEM((NV, 32, CW), BF16),
            pltpu.VMEM((NV, 32, CW), BF16),
            pltpu.VMEM((NV, 32, CW), BF16),
            pltpu.VMEM((NV, 32, CW), F32),
            pltpu.VMEM((NV, 32, CW), F32),
            pltpu.VMEM((32, DC), F32),
            pltpu.VMEM((NX, 128, 256), BF16),
            pltpu.VMEM((NX, 128, 128), BF16),
            pltpu.VMEM((NX - 1, 128, 256), BF16),
            pltpu.VMEM((NX - 1, 128, 128), BF16),
            pltpu.VMEM((NZ, S, 256), BF16),
            pltpu.VMEM((NZ, S, 128), BF16),
            pltpu.VMEM((NZ - 1, S, 256), BF16),
            pltpu.VMEM((NZ - 1, S, 128), BF16),
            pltpu.VMEM((NV, S, CW), BF16),
            pltpu.VMEM((S, KV), F32),
            pltpu.SemaphoreType.DMA((12,)),
            pltpu.SemaphoreType.DMA((N_COPIES,)),
            pltpu.SemaphoreType.DMA((N_COPIES,)),
        ],
        compiler_params=pltpu.CompilerParams(collective_id=0, has_side_effects=True, vmem_limit_bytes=60 << 20),
        cost_estimate=pl.CostEstimate(flops=500_000_000, bytes_accessed=3_000_000, transcendentals=0),
        name="sirt",
    )(
        volume, foot, column_footprint_weights, tile_rows, table_offset, view_angle,
        measured.reshape(32, DC), row_scale.reshape(32, DC), column_scale,
    )
    return pl.pallas_call(
        hand_over,
        out_shape=(jax.ShapeDtypeStruct((S, KV), F32), jax.ShapeDtypeStruct((4, 8, DC), F32)),
        in_specs=[hbm] * 2,
        out_specs=(hbm, hbm),
        scratch_shapes=[pltpu.VMEM((S, KV), F32), pltpu.VMEM((4, 8, DC), F32), pltpu.SemaphoreType.DMA((10,))],
        compiler_params=pltpu.CompilerParams(vmem_limit_bytes=60 << 20),
        name="hand_over",
    )(updated, weighted.reshape(4, 8, DC))


def solution(mesh):
    placed = (
        P(None, "vol"),
        P("view", "vol", None, None),
        P("vol", None),
        P("vol"),
        P("view"),
        P("view"),
        P("vol", "view", None),
        P("vol", "view", None),
        P(None, "vol"),
    )
    return jax.shard_map(
        body,
        mesh=mesh,
        in_specs=placed,
        out_specs=(P(None, "vol"), P("vol", "view", None)),
        check_vma=False,
    )
```

time: 59.6 us -> 47.6 us (0.80)
  local copies, waits for them, and re-layouts: 9.59 us -> 0 us
  Pallas kernels: 47.6 us -> 46.2 us
  other arithmetic: 0.73 us -> 0 us
    unnamed x13 -> x0, local copies, waits for them, and re-layouts: 8.69 us -> none
    pallas_call x1, Pallas kernels: 47.6 us -> 44.4 us  [body(): pl.pallas_call(kernel, out_shape=(jax.ShapeDtypeStruct((S, KV), F32), jax...]
    pallas_call x0 -> x1, Pallas kernels: none -> 1.8 us  [body(): pl.pallas_call(hand_over, out_shape=(jax.ShapeDtypeStruct((S, KV), F32),...]
    add x2 -> x0, other arithmetic: 0.73 us -> none  [body(): jnp.arange(8, dtype=jnp.int32)[:, None] * 1024 + starts[:, None]]
    reshape x1 -> x0, local copies, waits for them, and re-layouts: 0.73 us -> none  [body(): view_angle.reshape(8, 1)]
where the time goes in v2:
time: 47.6 us; the launch traced here: 47.5 us
  Pallas kernels  46.2 us (97%)
  between operations  1.29 us (3%)
    pallas_call x1, Pallas kernels, body(): pl.pallas_call(kernel, out_shape=(jax.ShapeDtypeStruct((S, KV), F32), jax...  44.4 us
    pallas_call x1, Pallas kernels, body(): pl.pallas_call(hand_over, out_shape=(jax.ShapeDtypeStruct((S, KV), F32),...  1.8 us

profile of v2, /device:TPU:1, one launch (start us, length us, event | category | flops | bytes accessed | tf_op | source)
XLA Modules:
  0.0 47.5 jit_solution(8213884763856062712)
XLA Ops:
  1.3 44.4 %sirt.1 = (f32[16,1024]{1,0:T(8,128)}, f32[32,3072]{1,0:T(8,128)}) custom-call(f32[16,1024]{1,0:T(8,128)} %vol_hbm.1, f32[8,16,80]{2,1,0:T(8,128)} %bitcast.9, bf16[1024,3072]{1,0:T(8,128)(2,1)} %c_hbm.1, s32[1]{0:T(128)S(6)} %copy.11.tile_hbm, s32[8]{0:T(128)} %offset_hbm.1, s32[8]{0:T(128)} %angle_hbm.1, f32[32,3072]{1,0:T(8,128)} %bitcast.7, ...), custom_call_target="tpu_custom_call" | custom-call | flops 500000000 | bytes 3000000 | tf_op jit(solution)/shard_map/sirt/pallas_call | solution.py:256
  45.7 1.8 %hand_over.1 = (f32[16,1024]{1,0:T(8,128)}, f32[4,8,3072]{2,1,0:T(8,128)}) custom-call(f32[16,1024]{1,0:T(8,128)} %get-tuple-element.4.upd_in, f32[4,8,3072]{2,1,0:T(8,128)} %bitcast.6), custom_call_target="tpu_custom_call" | custom-call | tf_op jit(solution)/shard_map/hand_over/pallas_call | solution.py:307

commit v3 on v2

--- a/solution.py
+++ b/solution.py
@@ -34,7 +34,7 @@
     upd_hbm, wtd_hbm,
     vol_ref, foot_ref, cs_ref, tile_s, offset_s, angle_s, cbuf, cfull, mraw, rraw, ybuf, pbuf, gbuf, gt, a4, acat, atb,
     msend, rsend, mrecv, rrecv, psend, precv, wout,
-    zsend0, zsend1, zrecv0, zrecv1, ssend0, ssend1, srecv0, srecv1, sall, ufin,
+    zsend0, zsend1, zrecv0, zrecv1, ssend0, ssend1, srecv0, srecv1, sall, uall, ufin,
     lsem, ssem, rsem,
 ):
     d = lax.axis_index("vol")
@@ -53,6 +53,9 @@
 
     def yp(o):
         return (d, lax.rem(y + o, NY) * 2 + c)
+
+    def vq(o, swap):
+        return (d, lax.rem(y + o, NY) * 2 + (1 - c if swap else c))
 
     def xyp(p, o):
         return (lax.rem(x + p, NX) * NZ + z, lax.rem(y + o, NY) * 2 + c)
@@ -170,46 +173,59 @@
 
     for copy in y_x:
         copy.wait_recv()
-    z_x = []
     for copy in exchanged:
         copy.wait_recv()
     for j, (first, width) in enumerate(CHUNKS):
         cols = pl.ds(first, width)
-        zsend, zrecv = ((zsend0, zrecv0), (zsend1, zrecv1))[j]
         proj = jnp.dot(acat[...], ybuf[:, :, cols].reshape(NX * NZ * S, width), preferred_element_type=F32)
         proj = proj[:256] + proj[256:]
         psend[:, :, cols] = proj.reshape(NV, 32, width)
         measured = mrecv[:, :, cols].astype(F32).reshape(256, width)
         weighted = rrecv[:, :, cols].astype(F32).reshape(256, width) * (measured - proj)
         part = jnp.dot(atb[...], weighted.astype(BF16), preferred_element_type=F32)
-        zsend[...] = part.astype(BF16).reshape(NX, 128, width)
-        z_x.append([send(zsend.at[lax.rem(x + o, NX)], zrecv.at[o - 1], xp(o)) for o in (2, 1, 3)])
+        part = part.astype(BF16)
+        if j == 0:
+            zsend0[...] = part.reshape(NX, 128, width)
+            z0_x = [send(zsend0.at[lax.rem(x + o, NX)], zrecv0.at[o - 1], xp(o)) for o in (2, 1, 3)]
+        else:
+            zsend1[...] = part.reshape(NX, NZ, S, width)
+            z1_z = [send(zsend1.at[:, lax.rem(z + o, NZ)], zrecv1.at[o - 1], zp(o)) for o in (4, 3, 5, 2, 6, 1, 7)]
 
     p_v = [send(psend.at[lax.rem(g + o, NV)], precv.at[g], vp(o)) for o in (1, 7, 2, 6, 3, 5, 4)]
     precv[g] = psend[g]
 
-    s_z = []
-    for j, (first, width) in enumerate(CHUNKS):
-        zsend, zrecv = ((zsend0, zrecv0), (zsend1, zrecv1))[j]
-        ssend, srecv = ((ssend0, srecv0), (ssend1, srecv1))[j]
-        for copy in z_x[j]:
-            copy.wait_recv()
-        total = zsend[x].astype(F32)
-        for o in range(NX - 1):
-            total += zrecv[o].astype(F32)
-        ssend[...] = total.astype(BF16).reshape(NZ, S, width)
-        s_z.append([send(ssend.at[lax.rem(z + o, NZ)], srecv.at[o - 1], zp(o)) for o in (4, 3, 5, 2, 6, 1, 7)])
-
-    for j, (first, width) in enumerate(CHUNKS):
-        ssend, srecv = ((ssend0, srecv0), (ssend1, srecv1))[j]
-        for copy in s_z[j]:
-            copy.wait_recv()
-        total = ssend[z].astype(F32)
-        for o in range(NZ - 1):
-            total += srecv[o].astype(F32)
-        sall[g, :, first : first + width] = total.astype(BF16)
-
-    s_v = {o: send(sall.at[g], sall.at[g], vp(o)) for o in (4, 3, 5, 2, 6, 1, 7)}
+    for copy in z0_x:
+        copy.wait_recv()
+    total = zsend0[x].astype(F32)
+    for o in range(NX - 1):
+        total += zrecv0[o].astype(F32)
+    ssend0[...] = total.astype(BF16).reshape(NZ, S, 256)
+    z0_z = [send(ssend0.at[lax.rem(z + o, NZ)], srecv0.at[o - 1], zp(o)) for o in (4, 3, 5, 2, 6, 1, 7)]
+
+    for copy in z1_z:
+        copy.wait_recv()
+    total = zsend1[:, z].astype(F32)
+    for o in range(NZ - 1):
+        total += zrecv1[o].astype(F32)
+    ssend1[...] = total.astype(BF16)
+    z1_x = [send(ssend1.at[lax.rem(x + o, NX)], srecv1.at[o - 1], xp(o)) for o in (2, 1, 3)]
+
+    for copy in z0_z:
+        copy.wait_recv()
+    total = ssend0[z].astype(F32)
+    for o in range(NZ - 1):
+        total += srecv0[o].astype(F32)
+    sall[g, :, :256] = total.astype(BF16)
+
+    for copy in z1_x:
+        copy.wait_recv()
+    total = ssend1[x].astype(F32)
+    for o in range(NX - 1):
+        total += srecv1[o].astype(F32)
+    sall[g, :, 256:] = total.astype(BF16)
+
+    s_v = {o: [send(sall.at[g], sall.at[g], vq(o, swap)) for swap in (False, True)] for o in (2, 1, 3)}
+    s_v[0] = send(sall.at[g], sall.at[g], core)
 
     for copy in p_v:
         copy.wait_recv()
@@ -222,12 +238,18 @@
 
     cfull_in.wait()
     cs_in.wait()
-
-    for copy in s_v.values():
-        copy.wait_recv()
-    both = jnp.concatenate([sall[k] for k in range(NV)], axis=1)
-    total = lax.dot_general(both, cfull[...], (((1,), (1,)), ((), ())), preferred_element_type=F32)
-
+    for o in (0, 1, 3, 2):
+        if not o:
+            s_v[0].wait_recv()
+        else:
+            for copy in s_v[o]:
+                copy.wait_recv()
+        group = lax.rem(y + NY - o, NY)
+        both = jnp.concatenate([sall[2 * group], sall[2 * group + 1]], axis=1)
+        weights = cfull[:, pl.ds(pl.multiple_of(group * 2 * CW, 128), 2 * CW)]
+        uall[group] = lax.dot_general(both, weights, (((1,), (1,)), ((), ())), preferred_element_type=F32)
+
+    total = ((uall[0] + uall[1]) + uall[2]) + uall[3]
     ufin[...] = vol_ref[...] + cs_ref[...] * total
     u_out = pltpu.make_async_copy(ufin, upd_hbm, lsem.at[11])
     u_out.start()
@@ -284,14 +306,15 @@
             pltpu.VMEM((NV, 32, CW), F32),
             pltpu.VMEM((32, DC), F32),
             pltpu.VMEM((NX, 128, 256), BF16),
-            pltpu.VMEM((NX, 128, 128), BF16),
+            pltpu.VMEM((NX, NZ, S, 128), BF16),
             pltpu.VMEM((NX - 1, 128, 256), BF16),
-            pltpu.VMEM((NX - 1, 128, 128), BF16),
+            pltpu.VMEM((NZ - 1, NX, S, 128), BF16),
             pltpu.VMEM((NZ, S, 256), BF16),
-            pltpu.VMEM((NZ, S, 128), BF16),
+            pltpu.VMEM((NX, S, 128), BF16),
             pltpu.VMEM((NZ - 1, S, 256), BF16),
-            pltpu.VMEM((NZ - 1, S, 128), BF16),
+            pltpu.VMEM((NX - 1, S, 128), BF16),
             pltpu.VMEM((NV, S, CW), BF16),
+            pltpu.VMEM((NY, S, KV), F32),
             pltpu.VMEM((S, KV), F32),
             pltpu.SemaphoreType.DMA((12,)),
             pltpu.SemaphoreType.DMA((N_COPIES,)),

time: 47.6 us -> 45.6 us (0.958)
  Pallas kernels: 46.2 us -> 44.2 us
    pallas_call x1, Pallas kernels: 44.4 us -> 42.4 us  [body(): pl.pallas_call(kernel, out_shape=(jax.ShapeDtypeStruct((S, KV), F32), jax...]
where the time goes in v3:
time: 45.6 us; the launch traced here: 45.5 us
  Pallas kernels  44.2 us (97%)
  between operations  1.29 us (3%)
    pallas_call x1, Pallas kernels, body(): pl.pallas_call(kernel, out_shape=(jax.ShapeDtypeStruct((S, KV), F32), jax...  42.4 us
    pallas_call x1, Pallas kernels, body(): pl.pallas_call(hand_over, out_shape=(jax.ShapeDtypeStruct((S, KV), F32),...  1.8 us

profile of v3, /device:TPU:1, one launch (start us, length us, event | category | flops | bytes accessed | tf_op | source)
XLA Modules:
  0.0 45.5 jit_solution(5674036598557469922)
XLA Ops:
  1.3 42.4 %sirt.1 = (f32[16,1024]{1,0:T(8,128)}, f32[32,3072]{1,0:T(8,128)}) custom-call(f32[16,1024]{1,0:T(8,128)} %vol_hbm.1, f32[8,16,80]{2,1,0:T(8,128)} %bitcast.9, bf16[1024,3072]{1,0:T(8,128)(2,1)} %c_hbm.1, s32[1]{0:T(128)S(6)} %copy.11.tile_hbm, s32[8]{0:T(128)} %offset_hbm.1, s32[8]{0:T(128)} %angle_hbm.1, f32[32,3072]{1,0:T(8,128)} %bitcast.7, ...), custom_call_target="tpu_custom_call" | custom-call | flops 500000000 | bytes 3000000 | tf_op jit(solution)/shard_map/sirt/pallas_call | solution.py:278
  43.6 1.8 %hand_over.1 = (f32[16,1024]{1,0:T(8,128)}, f32[4,8,3072]{2,1,0:T(8,128)}) custom-call(f32[16,1024]{1,0:T(8,128)} %get-tuple-element.4.upd_in, f32[4,8,3072]{2,1,0:T(8,128)} %bitcast.6), custom_call_target="tpu_custom_call" | custom-call | tf_op jit(solution)/shard_map/hand_over/pallas_call | solution.py:330

commit v4 on v3

--- a/solution.py
+++ b/solution.py
@@ -13,7 +13,11 @@
 NX, NY, NZ, NV = 4, 4, 8, 8
 CW = DC // 8
 CHUNKS = ((0, 256), (256, 128))
-N_COPIES = 160
+FAR_Z = (4, 3, 5, 2, 6, 1, 7)
+(FZ_S, M_S, R_S, Y1X_S, Y1Z_S, Y0Z_S, Y0X_S, F_S, _, FC_S, Z0X_S, Z1Z_S, Z0Z_S, Z1X_S, P_S, SV_S) = range(16)
+(FZ_R, M_R, R_R, Y1Z_R, Y0X_R, FC_R, Z0X_R, Z1Z_R, Z0Z_R, Z1X_R, P_R) = range(11)
+Y1X_R, Y0Z_R, F_R, SV_R = 11, 14, 21, 25
+N_SENT, N_ARRIVED = 16, 29
 
 
 def split2(a):
@@ -32,7 +36,7 @@
 def kernel(
     vol_hbm, foot_hbm, c_hbm, tile_hbm, offset_hbm, angle_hbm, m_hbm, r_hbm, cs_hbm,
     upd_hbm, wtd_hbm,
-    vol_ref, foot_ref, cs_ref, tile_s, offset_s, angle_s, cbuf, cfull, mraw, rraw, ybuf, pbuf, gbuf, gt, a4, acat, atb,
+    vol_ref, foot_ref, cs_ref, tile_s, offset_s, angle_s, cbuf, cfull, mraw, rraw, ybuf0, ybuf1, pbuf, gbuf, gt, a4, acat, atb,
     msend, rsend, mrecv, rrecv, psend, precv, wout,
     zsend0, zsend1, zrecv0, zrecv1, ssend0, ssend1, srecv0, srecv1, sall, uall, ufin,
     lsem, ssem, rsem,
@@ -62,19 +66,19 @@
 
     core = (d, y * 2 + (1 - c))
 
-    counter = [0]
-    started = []
-
-    def send(src, dst, device):
-        n = counter[0]
-        counter[0] += 1
-        copy = pltpu.make_async_remote_copy(
-            src_ref=src, dst_ref=dst, send_sem=ssem.at[n], recv_sem=rsem.at[n],
-            device_id=device, device_id_type=MESH,
+    def transfer(src, dst, device, s, r):
+        return pltpu.make_async_remote_copy(
+            src_ref=src, dst_ref=dst, send_sem=ssem.at[s], recv_sem=rsem.at[r], device_id=device, device_id_type=MESH
         )
-        copy.start()
-        started.append(copy)
-        return copy
+
+    def send(src, dst, device, s, r):
+        transfer(src, dst, device, s, r).start()
+
+    def arrived(ref, r):
+        transfer(ref, ref, core, 0, r).wait_recv()
+
+    def sent(ref, s):
+        transfer(ref, ref, core, s, 0).wait_send()
 
     barrier = pltpu.get_barrier_semaphore()
     partners = [xp(o) for o in range(1, NX)] + [zp(o) for o in range(1, NZ)] + [vp(o) for o in range(1, NV)]
@@ -117,12 +121,12 @@
 
     pl.semaphore_wait(barrier, len(partners))
 
-    f_z = [send(pbuf.at[lax.rem(z + o, NZ)], gbuf.at[z], zp(o)) for o in range(1, NZ)]
+    for o in range(1, NZ):
+        send(pbuf.at[lax.rem(z + o, NZ)], gbuf.at[z], zp(o), FZ_S, FZ_R)
     gbuf[z] = pbuf[z]
 
     shift_back = jnp.where(angle == 0, 0, DC - angle)
-    exchanged = []
-    for copy_in, raw, out, got in ((m_in, mraw, msend, mrecv), (r_in, rraw, rsend, rrecv)):
+    for copy_in, raw, out, got, s, r in ((m_in, mraw, msend, mrecv, M_S, M_R), (r_in, rraw, rsend, rrecv, R_S, R_R)):
         copy_in.wait()
         for i in range(0, 4, 2):
             rolled = [barrel(raw[8 * n : 8 * n + 8, :], shift_back) for n in (i, i + 1)]
@@ -130,54 +134,64 @@
             for k in range(NV):
                 out[k, 8 * i : 8 * i + 16, :] = rolled[:, k * CW : (k + 1) * CW]
         for o in (4, 3, 5, 2, 6, 1, 7):
-            exchanged.append(send(out.at[lax.rem(g + o, NV)], got.at[g], vp(o)))
+            send(out.at[lax.rem(g + o, NV)], got.at[g], vp(o), s, r)
         got[g] = out[g]
 
     vol_in.wait()
     v_all = jnp.concatenate(split2(vol_ref[...]), axis=0)
     c_in.wait()
     prod = jnp.dot(v_all, cbuf[...], preferred_element_type=F32)
-    ybuf[d] = (prod[:S] + prod[S:]).astype(BF16)
-    y_z = [send(ybuf.at[d], ybuf.at[d], zp(o)) for o in range(1, NZ)]
-    y_x = [send(ybuf.at[d], ybuf.at[d], xp(o)) for o in range(1, NX)]
+    own = (prod[:S] + prod[S:]).astype(BF16)
+    ybuf0[d] = own[:, :256]
+    ybuf1[d] = own[:, 256:]
+    for n, o in enumerate((2, 1, 3)):
+        send(ybuf1.at[d], ybuf1.at[d], xp(o), Y1X_S, Y1X_R + n)
+    for o in range(1, NZ):
+        send(ybuf0.at[d], ybuf0.at[d], zp(o), Y0Z_S, Y0Z_R + o - 1)
+    for o in (2, 1, 3):
+        send(ybuf0.at[d], ybuf0.at[d], xp(o), Y0X_S, Y0X_R)
+    for o in range(1, NZ):
+        send(ybuf1.at[d], ybuf1.at[d], zp(o), Y1Z_S, Y1Z_R)
     cfull_in.start()
 
-    for copy in f_z:
-        copy.wait_recv()
+    arrived(gbuf.at[pl.ds(0, NZ - 1)], FZ_R)
     turned = jnp.transpose(gbuf[...].reshape(NZ * S, 128))
     gt[...] = turned.reshape(NX, 32, 128)
-    f_xy = {}
     for p, o in [(p, o) for p in (0, 2, 1, 3) for o in (2, 1, 3, 0) if p or o]:
-        f_xy[p, o] = send(gt.at[lax.rem(x + p, NX)], a4.at[g, x], xyp(p, o))
-    a4[g, x] = gt[x]
-    f_c = [send(gt.at[x], a4.at[g, x], core)]
-
+        send(gt.at[lax.rem(x + p, NX)], a4.at[c, y, x], xyp(p, o), F_S + min(p, 1), F_R + p)
+    a4[c, y, x] = gt[x]
+
+    for n, o in enumerate((2, 1, 3)):
+        tile = lax.rem(x + NX - o, NX) * NZ + z
+        arrived(ybuf1.at[tile], Y1X_R + n)
+        for p in range(1, NZ):
+            send(ybuf1.at[tile], ybuf1.at[tile], zp(p), Y1Z_S, Y1Z_R)
     for o in range(1, NZ):
-        y_z[o - 1].wait_recv()
         tile = x * NZ + lax.rem(z + NZ - o, NZ)
-        y_x += [send(ybuf.at[tile], ybuf.at[tile], xp(p)) for p in range(1, NX)]
-
-    for (p, o), copy in f_xy.items():
-        copy.wait_recv()
-        piece = a4.at[lax.rem(y + NY - o, NY) * 2 + c, lax.rem(x + NX - p, NX)]
-        f_c.append(send(piece, piece, core))
-    for copy in f_c:
-        copy.wait_recv()
+        arrived(ybuf0.at[tile], Y0Z_R + o - 1)
+        for p in (2, 1, 3):
+            send(ybuf0.at[tile], ybuf0.at[tile], xp(p), Y0X_S, Y0X_R)
+
+    for p in (0, 2, 1, 3):
+        column = a4.at[c, :, lax.rem(x + NX - p, NX)]
+        arrived(column if p else a4.at[c, pl.ds(0, NY - 1), x], F_R + p)
+        send(column, column, core, FC_S, FC_R)
+    arrived(a4.at[1 - c], FC_R)
 
     for k in range(NX):
-        part = a4[:, k].reshape(NV * 32, 128)
+        part = jnp.concatenate([a4[v % 2, v // 2, k] for v in range(NV)], axis=0)
         hi, lo = split2(part)
         acat[0:256, k * 128 : (k + 1) * 128] = hi
         acat[256:512, k * 128 : (k + 1) * 128] = lo
         atb[k * 128 : (k + 1) * 128, :] = jnp.transpose(part).astype(BF16)
 
-    for copy in y_x:
-        copy.wait_recv()
-    for copy in exchanged:
-        copy.wait_recv()
+    arrived(ybuf0.at[pl.ds(0, NZ * (NX - 1))], Y0X_R)
+    arrived(ybuf1.at[pl.ds(0, NX * (NZ - 1))], Y1Z_R)
+    arrived(mrecv.at[pl.ds(0, NV - 1)], M_R)
+    arrived(rrecv.at[pl.ds(0, NV - 1)], R_R)
     for j, (first, width) in enumerate(CHUNKS):
         cols = pl.ds(first, width)
-        proj = jnp.dot(acat[...], ybuf[:, :, cols].reshape(NX * NZ * S, width), preferred_element_type=F32)
+        proj = jnp.dot(acat[...], (ybuf0, ybuf1)[j][...].reshape(NX * NZ * S, width), preferred_element_type=F32)
         proj = proj[:256] + proj[256:]
         psend[:, :, cols] = proj.reshape(NV, 32, width)
         measured = mrecv[:, :, cols].astype(F32).reshape(256, width)
@@ -186,49 +200,51 @@
         part = part.astype(BF16)
         if j == 0:
             zsend0[...] = part.reshape(NX, 128, width)
-            z0_x = [send(zsend0.at[lax.rem(x + o, NX)], zrecv0.at[o - 1], xp(o)) for o in (2, 1, 3)]
+            for o in (2, 1, 3):
+                send(zsend0.at[lax.rem(x + o, NX)], zrecv0.at[o - 1], xp(o), Z0X_S, Z0X_R)
         else:
             zsend1[...] = part.reshape(NX, NZ, S, width)
-            z1_z = [send(zsend1.at[:, lax.rem(z + o, NZ)], zrecv1.at[o - 1], zp(o)) for o in (4, 3, 5, 2, 6, 1, 7)]
-
-    p_v = [send(psend.at[lax.rem(g + o, NV)], precv.at[g], vp(o)) for o in (1, 7, 2, 6, 3, 5, 4)]
+            for o in FAR_Z:
+                send(zsend1.at[:, lax.rem(z + o, NZ)], zrecv1.at[o - 1], zp(o), Z1Z_S, Z1Z_R)
+
+    for o in (1, 7, 2, 6, 3, 5, 4):
+        send(psend.at[lax.rem(g + o, NV)], precv.at[g], vp(o), P_S, P_R)
     precv[g] = psend[g]
 
-    for copy in z0_x:
-        copy.wait_recv()
+    arrived(zrecv0, Z0X_R)
     total = zsend0[x].astype(F32)
     for o in range(NX - 1):
         total += zrecv0[o].astype(F32)
     ssend0[...] = total.astype(BF16).reshape(NZ, S, 256)
-    z0_z = [send(ssend0.at[lax.rem(z + o, NZ)], srecv0.at[o - 1], zp(o)) for o in (4, 3, 5, 2, 6, 1, 7)]
-
-    for copy in z1_z:
-        copy.wait_recv()
+    for o in FAR_Z:
+        send(ssend0.at[lax.rem(z + o, NZ)], srecv0.at[o - 1], zp(o), Z0Z_S, Z0Z_R)
+
+    arrived(zrecv1, Z1Z_R)
     total = zsend1[:, z].astype(F32)
     for o in range(NZ - 1):
         total += zrecv1[o].astype(F32)
     ssend1[...] = total.astype(BF16)
-    z1_x = [send(ssend1.at[lax.rem(x + o, NX)], srecv1.at[o - 1], xp(o)) for o in (2, 1, 3)]
-
-    for copy in z0_z:
-        copy.wait_recv()
+    for o in (2, 1, 3):
+        send(ssend1.at[lax.rem(x + o, NX)], srecv1.at[o - 1], xp(o), Z1X_S, Z1X_R)
+
+    arrived(srecv0, Z0Z_R)
     total = ssend0[z].astype(F32)
     for o in range(NZ - 1):
         total += srecv0[o].astype(F32)
     sall[g, :, :256] = total.astype(BF16)
 
-    for copy in z1_x:
-        copy.wait_recv()
+    arrived(srecv1, Z1X_R)
     total = ssend1[x].astype(F32)
     for o in range(NX - 1):
         total += srecv1[o].astype(F32)
     sall[g, :, 256:] = total.astype(BF16)
 
-    s_v = {o: [send(sall.at[g], sall.at[g], vq(o, swap)) for swap in (False, True)] for o in (2, 1, 3)}
-    s_v[0] = send(sall.at[g], sall.at[g], core)
-
-    for copy in p_v:
-        copy.wait_recv()
+    for o in (2, 1, 3):
+        for swap in (False, True):
+            send(sall.at[g], sall.at[g], vq(o, swap), SV_S, SV_R + o)
+    send(sall.at[g], sall.at[g], core, SV_S, SV_R)
+
+    arrived(precv.at[pl.ds(0, NV - 1)], P_R)
     for i in range(4):
         rows = slice(8 * i, 8 * i + 8)
         row = jnp.concatenate([precv[k, rows, :] for k in range(NV)], axis=1)
@@ -239,11 +255,7 @@
     cfull_in.wait()
     cs_in.wait()
     for o in (0, 1, 3, 2):
-        if not o:
-            s_v[0].wait_recv()
-        else:
-            for copy in s_v[o]:
-                copy.wait_recv()
+        arrived(sall.at[pl.ds(0, 2 if o else 1)], SV_R + o)
         group = lax.rem(y + NY - o, NY)
         both = jnp.concatenate([sall[2 * group], sall[2 * group + 1]], axis=1)
         weights = cfull[:, pl.ds(pl.multiple_of(group * 2 * CW, 128), 2 * CW)]
@@ -253,19 +265,26 @@
     ufin[...] = vol_ref[...] + cs_ref[...] * total
     u_out = pltpu.make_async_copy(ufin, upd_hbm, lsem.at[11])
     u_out.start()
-    for copy in started:
-        copy.wait_send()
+    for ref, s in (
+        (gbuf.at[pl.ds(0, NZ - 1)], FZ_S), (mrecv.at[pl.ds(0, NV - 1)], M_S), (rrecv.at[pl.ds(0, NV - 1)], R_S),
+        (ybuf1.at[pl.ds(0, NX - 1)], Y1X_S), (ybuf1.at[pl.ds(0, NX * (NZ - 1))], Y1Z_S),
+        (ybuf0.at[pl.ds(0, NZ - 1)], Y0Z_S), (ybuf0.at[pl.ds(0, NZ * (NX - 1))], Y0X_S),
+        (a4.at[0, 0, pl.ds(0, 3)], F_S), (a4.at[0, :, pl.ds(0, 3)], F_S + 1), (a4.at[0], FC_S),
+        (zrecv0, Z0X_S), (zrecv1, Z1Z_S), (srecv0, Z0Z_S), (srecv1, Z1X_S),
+        (precv.at[pl.ds(0, NV - 1)], P_S), (sall.at[pl.ds(0, NV - 1)], SV_S),
+    ):
+        sent(ref, s)
     w_out.wait()
     u_out.wait()
 
 
 def hand_over(upd_in, wtd_in, upd_out, wtd_out, upd_held, wtd_held, sem):
-    pieces = [(upd_in, upd_held, upd_out)] + [(wtd_in.at[i], wtd_held.at[i], wtd_out.at[i]) for i in range(4)]
+    pieces = ((wtd_in, wtd_held, wtd_out), (upd_in, upd_held, upd_out))
     arriving = [pltpu.make_async_copy(src, held, sem.at[n]) for n, (src, held, _) in enumerate(pieces)]
-    leaving = [pltpu.make_async_copy(held, dst, sem.at[5 + n]) for n, (_, held, dst) in enumerate(pieces)]
+    leaving = [pltpu.make_async_copy(held, dst, sem.at[2 + n]) for n, (_, held, dst) in enumerate(pieces)]
     for copy in arriving:
         copy.start()
-    for n in range(5):
+    for n in range(2):
         arriving[n].wait()
         leaving[n].start()
     for copy in leaving:
@@ -291,11 +310,12 @@
             pltpu.VMEM((KV, DC), BF16),
             pltpu.VMEM((32, DC), F32),
             pltpu.VMEM((32, DC), F32),
-            pltpu.VMEM((32, S, CW), BF16),
+            pltpu.VMEM((32, S, 256), BF16),
+            pltpu.VMEM((32, S, 128), BF16),
             pltpu.VMEM((NZ, S, 128), F32),
             pltpu.VMEM((NZ, S, 128), F32),
             pltpu.VMEM((NX, 32, 128), F32),
-            pltpu.VMEM((NV, NX, 32, 128), F32),
+            pltpu.VMEM((2, NY, NX, 32, 128), F32),
             pltpu.VMEM((512, 512), BF16),
             pltpu.VMEM((512, 256), BF16),
             pltpu.VMEM((NV, 32, CW), BF16),
@@ -317,8 +337,8 @@
             pltpu.VMEM((NY, S, KV), F32),
             pltpu.VMEM((S, KV), F32),
             pltpu.SemaphoreType.DMA((12,)),
-            pltpu.SemaphoreType.DMA((N_COPIES,)),
-            pltpu.SemaphoreType.DMA((N_COPIES,)),
+            pltpu.SemaphoreType.DMA((N_SENT,)),
+            pltpu.SemaphoreType.DMA((N_ARRIVED,)),
         ],
         compiler_params=pltpu.CompilerParams(collective_id=0, has_side_effects=True, vmem_limit_bytes=60 << 20),
         cost_estimate=pl.CostEstimate(flops=500_000_000, bytes_accessed=3_000_000, transcendentals=0),
@@ -332,7 +352,7 @@
         out_shape=(jax.ShapeDtypeStruct((S, KV), F32), jax.ShapeDtypeStruct((4, 8, DC), F32)),
         in_specs=[hbm] * 2,
         out_specs=(hbm, hbm),
-        scratch_shapes=[pltpu.VMEM((S, KV), F32), pltpu.VMEM((4, 8, DC), F32), pltpu.SemaphoreType.DMA((10,))],
+        scratch_shapes=[pltpu.VMEM((S, KV), F32), pltpu.VMEM((4, 8, DC), F32), pltpu.SemaphoreType.DMA((4,))],
         compiler_params=pltpu.CompilerParams(vmem_limit_bytes=60 << 20),
         name="hand_over",
     )(updated, weighted.reshape(4, 8, DC))

time: 45.6 us -> 42.8 us (0.939)
  Pallas kernels: 44.2 us -> 41.4 us
    pallas_call x1, Pallas kernels: 42.4 us -> 39.6 us  [body(): pl.pallas_call(kernel, out_shape=(jax.ShapeDtypeStruct((S, KV), F32), jax...]
where the time goes in v4:
time: 42.8 us; the launch traced here: 42.7 us
  Pallas kernels  41.4 us (97%)
  between operations  1.29 us (3%)
    pallas_call x1, Pallas kernels, body(): pl.pallas_call(kernel, out_shape=(jax.ShapeDtypeStruct((S, KV), F32), jax...  39.6 us
    pallas_call x1, Pallas kernels, body(): pl.pallas_call(hand_over, out_shape=(jax.ShapeDtypeStruct((S, KV), F32),...  1.79 us

profile of v4, /device:TPU:1, one launch (start us, length us, event | category | flops | bytes accessed | tf_op | source)
XLA Modules:
  0.0 42.7 jit_solution(10581560006951809620)
XLA Ops:
  1.3 39.6 %sirt.1 = (f32[16,1024]{1,0:T(8,128)}, f32[32,3072]{1,0:T(8,128)}) custom-call(f32[16,1024]{1,0:T(8,128)} %vol_hbm.1, f32[8,16,80]{2,1,0:T(8,128)} %bitcast.9, bf16[1024,3072]{1,0:T(8,128)(2,1)} %c_hbm.1, s32[1]{0:T(128)S(6)} %copy.11.tile_hbm, s32[8]{0:T(128)} %offset_hbm.1, s32[8]{0:T(128)} %angle_hbm.1, f32[32,3072]{1,0:T(8,128)} %bitcast.7, ...), custom_call_target="tpu_custom_call" | custom-call | flops 500000000 | bytes 3000000 | tf_op jit(solution)/shard_map/sirt/pallas_call | solution.py:297
  40.9 1.8 %hand_over.1 = (f32[16,1024]{1,0:T(8,128)}, f32[4,8,3072]{2,1,0:T(8,128)}) custom-call(f32[16,1024]{1,0:T(8,128)} %get-tuple-element.4.upd_in, f32[4,8,3072]{2,1,0:T(8,128)} %bitcast.6), custom_call_target="tpu_custom_call" | custom-call | tf_op jit(solution)/shard_map/hand_over/pallas_call | solution.py:350

commit v5 on v4

--- a/solution.py
+++ b/solution.py
@@ -117,25 +117,14 @@
         wanted = jnp.where((wanted >= 0) & (wanted < FR), wanted + (lane % 8) * 128, -1)
         one_hot = (source == wanted).astype(F32).astype(BF16)
         placed = lax.dot_general(f_all, one_hot, (((1,), (1,)), ((), ())), preferred_element_type=F32)
-        pbuf[zz] = placed[:S] + placed[S:]
+        placed = placed[:S] + placed[S:]
+        pbuf[zz] = (placed * placed).astype(BF16)
 
     pl.semaphore_wait(barrier, len(partners))
 
     for o in range(1, NZ):
         send(pbuf.at[lax.rem(z + o, NZ)], gbuf.at[z], zp(o), FZ_S, FZ_R)
     gbuf[z] = pbuf[z]
-
-    shift_back = jnp.where(angle == 0, 0, DC - angle)
-    for copy_in, raw, out, got, s, r in ((m_in, mraw, msend, mrecv, M_S, M_R), (r_in, rraw, rsend, rrecv, R_S, R_R)):
-        copy_in.wait()
-        for i in range(0, 4, 2):
-            rolled = [barrel(raw[8 * n : 8 * n + 8, :], shift_back) for n in (i, i + 1)]
-            rolled = jnp.concatenate(rolled, axis=0).astype(BF16)
-            for k in range(NV):
-                out[k, 8 * i : 8 * i + 16, :] = rolled[:, k * CW : (k + 1) * CW]
-        for o in (4, 3, 5, 2, 6, 1, 7):
-            send(out.at[lax.rem(g + o, NV)], got.at[g], vp(o), s, r)
-        got[g] = out[g]
 
     vol_in.wait()
     v_all = jnp.concatenate(split2(vol_ref[...]), axis=0)
@@ -152,11 +141,23 @@
         send(ybuf0.at[d], ybuf0.at[d], xp(o), Y0X_S, Y0X_R)
     for o in range(1, NZ):
         send(ybuf1.at[d], ybuf1.at[d], zp(o), Y1Z_S, Y1Z_R)
+
+    shift_back = jnp.where(angle == 0, 0, DC - angle)
+    for copy_in, raw, out, got, s, r in ((m_in, mraw, msend, mrecv, M_S, M_R), (r_in, rraw, rsend, rrecv, R_S, R_R)):
+        copy_in.wait()
+        for i in range(0, 4, 2):
+            rolled = [barrel(raw[8 * n : 8 * n + 8, :], shift_back) for n in (i, i + 1)]
+            rolled = jnp.concatenate(rolled, axis=0).astype(BF16)
+            for k in range(NV):
+                out[k, 8 * i : 8 * i + 16, :] = rolled[:, k * CW : (k + 1) * CW]
+        for o in (4, 3, 5, 2, 6, 1, 7):
+            send(out.at[lax.rem(g + o, NV)], got.at[g], vp(o), s, r)
+        got[g] = out[g]
     cfull_in.start()
 
     arrived(gbuf.at[pl.ds(0, NZ - 1)], FZ_R)
-    turned = jnp.transpose(gbuf[...].reshape(NZ * S, 128))
-    gt[...] = turned.reshape(NX, 32, 128)
+    turned = jnp.transpose(gbuf[...].astype(F32).reshape(NZ * S, 128))
+    gt[...] = turned.astype(BF16).reshape(NX, 32, 128)
     for p, o in [(p, o) for p in (0, 2, 1, 3) for o in (2, 1, 3, 0) if p or o]:
         send(gt.at[lax.rem(x + p, NX)], a4.at[c, y, x], xyp(p, o), F_S + min(p, 1), F_R + p)
     a4[c, y, x] = gt[x]
@@ -179,7 +180,7 @@
     arrived(a4.at[1 - c], FC_R)
 
     for k in range(NX):
-        part = jnp.concatenate([a4[v % 2, v // 2, k] for v in range(NV)], axis=0)
+        part = jnp.sqrt(jnp.concatenate([a4[v % 2, v // 2, k] for v in range(NV)], axis=0).astype(F32))
         hi, lo = split2(part)
         acat[0:256, k * 128 : (k + 1) * 128] = hi
         acat[256:512, k * 128 : (k + 1) * 128] = lo
@@ -312,10 +313,10 @@
             pltpu.VMEM((32, DC), F32),
             pltpu.VMEM((32, S, 256), BF16),
             pltpu.VMEM((32, S, 128), BF16),
-            pltpu.VMEM((NZ, S, 128), F32),
-            pltpu.VMEM((NZ, S, 128), F32),
-            pltpu.VMEM((NX, 32, 128), F32),
-            pltpu.VMEM((2, NY, NX, 32, 128), F32),
+            pltpu.VMEM((NZ, S, 128), BF16),
+            pltpu.VMEM((NZ, S, 128), BF16),
+            pltpu.VMEM((NX, 32, 128), BF16),
+            pltpu.VMEM((2, NY, NX, 32, 128), BF16),
             pltpu.VMEM((512, 512), BF16),
             pltpu.VMEM((512, 256), BF16),
             pltpu.VMEM((NV, 32, CW), BF16),

time: 42.8 us -> 41.2 us (0.963)
  Pallas kernels: 41.4 us -> 39.8 us
    pallas_call x1, Pallas kernels: 39.6 us -> 38 us  [body(): pl.pallas_call(kernel, out_shape=(jax.ShapeDtypeStruct((S, KV), F32), jax...]
where the time goes in v5:
time: 41.2 us; the launch traced here: 41.1 us
  Pallas kernels  39.8 us (97%)
  between operations  1.29 us (3%)
    pallas_call x1, Pallas kernels, body(): pl.pallas_call(kernel, out_shape=(jax.ShapeDtypeStruct((S, KV), F32), jax...  38 us
    pallas_call x1, Pallas kernels, body(): pl.pallas_call(hand_over, out_shape=(jax.ShapeDtypeStruct((S, KV), F32),...  1.79 us

profile of v5, /device:TPU:1, one launch (start us, length us, event | category | flops | bytes accessed | tf_op | source)
XLA Modules:
  0.0 41.1 jit_solution(4624240325811358796)
XLA Ops:
  1.3 38.0 %sirt.1 = (f32[16,1024]{1,0:T(8,128)}, f32[32,3072]{1,0:T(8,128)}) custom-call(f32[16,1024]{1,0:T(8,128)} %vol_hbm.1, f32[8,16,80]{2,1,0:T(8,128)} %bitcast.9, bf16[1024,3072]{1,0:T(8,128)(2,1)} %c_hbm.1, s32[1]{0:T(128)S(6)} %copy.11.tile_hbm, s32[8]{0:T(128)} %offset_hbm.1, s32[8]{0:T(128)} %angle_hbm.1, f32[32,3072]{1,0:T(8,128)} %bitcast.7, ...), custom_call_target="tpu_custom_call" | custom-call | flops 500000000 | bytes 3000000 | tf_op jit(solution)/shard_map/sirt/pallas_call | solution.py:298
  39.3 1.8 %hand_over.1 = (f32[16,1024]{1,0:T(8,128)}, f32[4,8,3072]{2,1,0:T(8,128)}) custom-call(f32[16,1024]{1,0:T(8,128)} %get-tuple-element.4.upd_in, f32[4,8,3072]{2,1,0:T(8,128)} %bitcast.6), custom_call_target="tpu_custom_call" | custom-call | tf_op jit(solution)/shard_map/hand_over/pallas_call | solution.py:351

commit v6 on v5

--- a/solution.py
+++ b/solution.py
@@ -35,10 +35,10 @@
 
 def kernel(
     vol_hbm, foot_hbm, c_hbm, tile_hbm, offset_hbm, angle_hbm, m_hbm, r_hbm, cs_hbm,
-    upd_hbm, wtd_hbm,
+    upd_ref, wtd_ref,
     vol_ref, foot_ref, cs_ref, tile_s, offset_s, angle_s, cbuf, cfull, mraw, rraw, ybuf0, ybuf1, pbuf, gbuf, gt, a4, acat, atb,
-    msend, rsend, mrecv, rrecv, psend, precv, wout,
-    zsend0, zsend1, zrecv0, zrecv1, ssend0, ssend1, srecv0, srecv1, sall, uall, ufin,
+    msend, rsend, mrecv, rrecv, psend, precv,
+    zsend0, zsend1, zrecv0, zrecv1, ssend0, ssend1, srecv0, srecv1, sall, uall,
     lsem, ssem, rsem,
 ):
     d = lax.axis_index("vol")
@@ -249,9 +249,7 @@
     for i in range(4):
         rows = slice(8 * i, 8 * i + 8)
         row = jnp.concatenate([precv[k, rows, :] for k in range(NV)], axis=1)
-        wout[rows, :] = rraw[rows, :] * (mraw[rows, :] - barrel(row, angle))
-    w_out = pltpu.make_async_copy(wout, wtd_hbm, lsem.at[10])
-    w_out.start()
+        wtd_ref[rows, :] = rraw[rows, :] * (mraw[rows, :] - barrel(row, angle))
 
     cfull_in.wait()
     cs_in.wait()
@@ -263,9 +261,7 @@
         uall[group] = lax.dot_general(both, weights, (((1,), (1,)), ((), ())), preferred_element_type=F32)
 
     total = ((uall[0] + uall[1]) + uall[2]) + uall[3]
-    ufin[...] = vol_ref[...] + cs_ref[...] * total
-    u_out = pltpu.make_async_copy(ufin, upd_hbm, lsem.at[11])
-    u_out.start()
+    upd_ref[...] = vol_ref[...] + cs_ref[...] * total
     for ref, s in (
         (gbuf.at[pl.ds(0, NZ - 1)], FZ_S), (mrecv.at[pl.ds(0, NV - 1)], M_S), (rrecv.at[pl.ds(0, NV - 1)], R_S),
         (ybuf1.at[pl.ds(0, NX - 1)], Y1X_S), (ybuf1.at[pl.ds(0, NX * (NZ - 1))], Y1Z_S),
@@ -275,31 +271,25 @@
         (precv.at[pl.ds(0, NV - 1)], P_S), (sall.at[pl.ds(0, NV - 1)], SV_S),
     ):
         sent(ref, s)
-    w_out.wait()
-    u_out.wait()
-
-
-def hand_over(upd_in, wtd_in, upd_out, wtd_out, upd_held, wtd_held, sem):
-    pieces = ((wtd_in, wtd_held, wtd_out), (upd_in, upd_held, upd_out))
-    arriving = [pltpu.make_async_copy(src, held, sem.at[n]) for n, (src, held, _) in enumerate(pieces)]
-    leaving = [pltpu.make_async_copy(held, dst, sem.at[2 + n]) for n, (_, held, dst) in enumerate(pieces)]
-    for copy in arriving:
+
+
+def hand_over(upd_in, wtd_in, upd_out, wtd_out, sem):
+    copies = (pltpu.make_async_copy(wtd_in, wtd_out, sem.at[0]), pltpu.make_async_copy(upd_in, upd_out, sem.at[1]))
+    for copy in copies:
         copy.start()
-    for n in range(2):
-        arriving[n].wait()
-        leaving[n].start()
-    for copy in leaving:
+    for copy in copies:
         copy.wait()
 
 
 def body(volume, row_footprint, column_footprint_weights, tile_rows, table_offset, view_angle, measured, row_scale, column_scale):
     foot = jnp.transpose(row_footprint[:, 0], (0, 2, 1))
     hbm = pl.BlockSpec(memory_space=pltpu.HBM)
+    vmem = pl.BlockSpec(memory_space=pltpu.VMEM)
     updated, weighted = pl.pallas_call(
         kernel,
-        out_shape=(jax.ShapeDtypeStruct((S, KV), F32), jax.ShapeDtypeStruct((32, DC), F32)),
+        out_shape=(pltpu.VMEM((S, KV), F32), pltpu.VMEM((32, DC), F32)),
         in_specs=[hbm] * 9,
-        out_specs=(hbm, hbm),
+        out_specs=(vmem, vmem),
         scratch_shapes=[
             pltpu.VMEM((S, KV), F32),
             pltpu.VMEM((8, S, FR), F32),
@@ -325,7 +315,6 @@
             pltpu.VMEM((NV, 32, CW), BF16),
             pltpu.VMEM((NV, 32, CW), F32),
             pltpu.VMEM((NV, 32, CW), F32),
-            pltpu.VMEM((32, DC), F32),
             pltpu.VMEM((NX, 128, 256), BF16),
             pltpu.VMEM((NX, NZ, S, 128), BF16),
             pltpu.VMEM((NX - 1, 128, 256), BF16),
@@ -336,8 +325,7 @@
             pltpu.VMEM((NX - 1, S, 128), BF16),
             pltpu.VMEM((NV, S, CW), BF16),
             pltpu.VMEM((NY, S, KV), F32),
-            pltpu.VMEM((S, KV), F32),
-            pltpu.SemaphoreType.DMA((12,)),
+            pltpu.SemaphoreType.DMA((10,)),
             pltpu.SemaphoreType.DMA((N_SENT,)),
             pltpu.SemaphoreType.DMA((N_ARRIVED,)),
         ],
@@ -351,10 +339,10 @@
     return pl.pallas_call(
         hand_over,
         out_shape=(jax.ShapeDtypeStruct((S, KV), F32), jax.ShapeDtypeStruct((4, 8, DC), F32)),
-        in_specs=[hbm] * 2,
+        in_specs=[vmem] * 2,
         out_specs=(hbm, hbm),
-        scratch_shapes=[pltpu.VMEM((S, KV), F32), pltpu.VMEM((4, 8, DC), F32), pltpu.SemaphoreType.DMA((4,))],
-        compiler_params=pltpu.CompilerParams(vmem_limit_bytes=60 << 20),
+        scratch_shapes=[pltpu.SemaphoreType.DMA((2,))],
+        compiler_params=pltpu.CompilerParams(vmem_limit_bytes=4 << 20),
         name="hand_over",
     )(updated, weighted.reshape(4, 8, DC))
 

time: 41.2 us -> 39.5 us (0.959)
  Pallas kernels: 39.8 us -> 38.2 us
    pallas_call x1, Pallas kernels: 1.79 us -> 0.78 us  [body(): pl.pallas_call(hand_over, out_shape=(jax.ShapeDtypeStruct((S, KV), F32),...]
    pallas_call x1, Pallas kernels: 38 us -> 37.4 us  [body(): pl.pallas_call(kernel, out_shape=(pltpu.VMEM((S, KV), F32), pltpu.VMEM((3...]
where the time goes in v6:
time: 39.5 us; the launch traced here: 39.4 us
  Pallas kernels  38.2 us (97%)
  between operations  1.29 us (3%)
    pallas_call x1, Pallas kernels, body(): pl.pallas_call(kernel, out_shape=(pltpu.VMEM((S, KV), F32), pltpu.VMEM((3...  37.4 us

profile of v6, /device:TPU:1, one launch (start us, length us, event | category | flops | bytes accessed | tf_op | source)
XLA Modules:
  0.0 39.4 jit_solution(17769311216970916425)
XLA Ops:
  1.3 37.4 %sirt.1 = (f32[16,1024]{1,0:T(8,128)S(1)}, f32[32,3072]{1,0:T(8,128)S(1)}) custom-call(f32[16,1024]{1,0:T(8,128)} %vol_hbm.1, f32[8,16,80]{2,1,0:T(8,128)} %bitcast.9, bf16[1024,3072]{1,0:T(8,128)(2,1)} %c_hbm.1, s32[1]{0:T(128)S(6)} %copy.11.tile_hbm, s32[8]{0:T(128)} %offset_hbm.1, s32[8]{0:T(128)} %angle_hbm.1, f32[32,3072]{1,0:T(8,128)} %bitcast.7, ...), custom_call_target="tpu_custom_call" | custom-call | flops 500000000 | bytes 3000000 | tf_op jit(solution)/shard_map/sirt/pallas_call | solution.py:288
  38.7 0.8 %hand_over.1 = (f32[16,1024]{1,0:T(8,128)}, f32[4,8,3072]{2,1,0:T(8,128)}) custom-call(f32[16,1024]{1,0:T(8,128)S(1)} %get-tuple-element.4.upd_in, f32[4,8,3072]{2,1,0:T(8,128)S(1)} %bitcast.6), custom_call_target="tpu_custom_call" | custom-call | tf_op jit(solution)/shard_map/hand_over/pallas_call | solution.py:339

commit v7 on v6

--- a/solution.py
+++ b/solution.py
@@ -36,7 +36,7 @@
 def kernel(
     vol_hbm, foot_hbm, c_hbm, tile_hbm, offset_hbm, angle_hbm, m_hbm, r_hbm, cs_hbm,
     upd_ref, wtd_ref,
-    vol_ref, foot_ref, cs_ref, tile_s, offset_s, angle_s, cbuf, cfull, mraw, rraw, ybuf0, ybuf1, pbuf, gbuf, gt, a4, acat, atb,
+    vol_ref, foot_ref, cs_ref, tile_s, offset_s, angle_s, cbuf, cfull, cturned, mraw, rraw, ybuf0, ybuf1, pbuf, gbuf, gt, a4, acat, atb,
     msend, rsend, mrecv, rrecv, psend, precv,
     zsend0, zsend1, zrecv0, zrecv1, ssend0, ssend1, srecv0, srecv1, sall, uall,
     lsem, ssem, rsem,
@@ -172,6 +172,14 @@
         arrived(ybuf0.at[tile], Y0Z_R + o - 1)
         for p in (2, 1, 3):
             send(ybuf0.at[tile], ybuf0.at[tile], xp(p), Y0X_S, Y0X_R)
+
+    def turn(block, carry):
+        cols = pl.ds(pl.multiple_of(block * 128, 128), 128)
+        cturned[cols, :] = jnp.transpose(cfull[:, cols])
+        return carry
+
+    cfull_in.wait()
+    lax.fori_loop(0, 8, turn, 0)
 
     for p in (0, 2, 1, 3):
         column = a4.at[c, :, lax.rem(x + NX - p, NX)]
@@ -212,6 +220,8 @@
         send(psend.at[lax.rem(g + o, NV)], precv.at[g], vp(o), P_S, P_R)
     precv[g] = psend[g]
 
+    lax.fori_loop(8, 18, turn, 0)
+
     arrived(zrecv0, Z0X_R)
     total = zsend0[x].astype(F32)
     for o in range(NX - 1):
@@ -228,6 +238,8 @@
     for o in (2, 1, 3):
         send(ssend1.at[lax.rem(x + o, NX)], srecv1.at[o - 1], xp(o), Z1X_S, Z1X_R)
 
+    lax.fori_loop(18, DC // 128, turn, 0)
+
     arrived(srecv0, Z0Z_R)
     total = ssend0[z].astype(F32)
     for o in range(NZ - 1):
@@ -251,14 +263,13 @@
         row = jnp.concatenate([precv[k, rows, :] for k in range(NV)], axis=1)
         wtd_ref[rows, :] = rraw[rows, :] * (mraw[rows, :] - barrel(row, angle))
 
-    cfull_in.wait()
     cs_in.wait()
     for o in (0, 1, 3, 2):
         arrived(sall.at[pl.ds(0, 2 if o else 1)], SV_R + o)
         group = lax.rem(y + NY - o, NY)
         both = jnp.concatenate([sall[2 * group], sall[2 * group + 1]], axis=1)
-        weights = cfull[:, pl.ds(pl.multiple_of(group * 2 * CW, 128), 2 * CW)]
-        uall[group] = lax.dot_general(both, weights, (((1,), (1,)), ((), ())), preferred_element_type=F32)
+        weights = cturned[pl.ds(pl.multiple_of(group * 2 * CW, 128), 2 * CW), :]
+        uall[group] = jnp.dot(both, weights, preferred_element_type=F32)
 
     total = ((uall[0] + uall[1]) + uall[2]) + uall[3]
     upd_ref[...] = vol_ref[...] + cs_ref[...] * total
@@ -299,6 +310,7 @@
             pltpu.SMEM((8,), jnp.int32),
             pltpu.VMEM((KV, CW), BF16),
             pltpu.VMEM((KV, DC), BF16),
+            pltpu.VMEM((DC, KV), BF16),
             pltpu.VMEM((32, DC), F32),
             pltpu.VMEM((32, DC), F32),
             pltpu.VMEM((32, S, 256), BF16),

time: 39.5 us -> 39 us (0.987)
  Pallas kernels: 38.2 us -> 37.5 us
    pallas_call x1, Pallas kernels: 37.4 us -> 36.8 us  [body(): pl.pallas_call(kernel, out_shape=(pltpu.VMEM((S, KV), F32), pltpu.VMEM((3...]
where the time goes in v7:
time: 39 us; the launch traced here: 38.8 us
  Pallas kernels  37.5 us (96%)
  between operations  1.29 us (3%)
    pallas_call x1, Pallas kernels, body(): pl.pallas_call(kernel, out_shape=(pltpu.VMEM((S, KV), F32), pltpu.VMEM((3...  36.8 us

profile of v7, /device:TPU:1, one launch (start us, length us, event | category | flops | bytes accessed | tf_op | source)
XLA Modules:
  0.0 38.8 jit_solution(2411270210236217668)
XLA Ops:
  1.3 36.8 %sirt.1 = (f32[16,1024]{1,0:T(8,128)S(1)}, f32[32,3072]{1,0:T(8,128)S(1)}) custom-call(f32[16,1024]{1,0:T(8,128)} %vol_hbm.1, f32[8,16,80]{2,1,0:T(8,128)} %bitcast.9, bf16[1024,3072]{1,0:T(8,128)(2,1)} %c_hbm.1, s32[1]{0:T(128)S(6)} %copy.11.tile_hbm, s32[8]{0:T(128)} %offset_hbm.1, s32[8]{0:T(128)} %angle_hbm.1, f32[32,3072]{1,0:T(8,128)} %bitcast.7, ...), custom_call_target="tpu_custom_call" | custom-call | flops 500000000 | bytes 3000000 | tf_op jit(solution)/shard_map/sirt/pallas_call | solution.py:299
  38.0 0.8 %hand_over.1 = (f32[16,1024]{1,0:T(8,128)}, f32[4,8,3072]{2,1,0:T(8,128)}) custom-call(f32[16,1024]{1,0:T(8,128)S(1)} %get-tuple-element.4.upd_in, f32[4,8,3072]{2,1,0:T(8,128)S(1)} %bitcast.6), custom_call_target="tpu_custom_call" | custom-call | tf_op jit(solution)/shard_map/hand_over/pallas_call | solution.py:351

commit v8 on v7

--- a/solution.py
+++ b/solution.py
@@ -12,12 +12,12 @@
 S, FR, DR, DC, KV = 16, 80, 128, 3072, 1024
 NX, NY, NZ, NV = 4, 4, 8, 8
 CW = DC // 8
-CHUNKS = ((0, 256), (256, 128))
+CHUNKS = ((0, 128), (128, 128), (256, 128))
 FAR_Z = (4, 3, 5, 2, 6, 1, 7)
 (FZ_S, M_S, R_S, Y1X_S, Y1Z_S, Y0Z_S, Y0X_S, F_S, _, FC_S, Z0X_S, Z1Z_S, Z0Z_S, Z1X_S, P_S, SV_S) = range(16)
 (FZ_R, M_R, R_R, Y1Z_R, Y0X_R, FC_R, Z0X_R, Z1Z_R, Z0Z_R, Z1X_R, P_R) = range(11)
-Y1X_R, Y0Z_R, F_R, SV_R = 11, 14, 21, 25
-N_SENT, N_ARRIVED = 16, 29
+Y1X_R, Y0Z_R, F_R, SV_R, Z0XB_R, Z0ZB_R = 11, 14, 21, 25, 29, 30
+N_SENT, N_ARRIVED = 16, 31
 
 
 def split2(a):
@@ -200,17 +200,17 @@
     arrived(rrecv.at[pl.ds(0, NV - 1)], R_R)
     for j, (first, width) in enumerate(CHUNKS):
         cols = pl.ds(first, width)
-        proj = jnp.dot(acat[...], (ybuf0, ybuf1)[j][...].reshape(NX * NZ * S, width), preferred_element_type=F32)
+        proj = jnp.dot(acat[...], (ybuf1[...] if j == 2 else ybuf0[:, :, cols]).reshape(NX * NZ * S, width), preferred_element_type=F32)
         proj = proj[:256] + proj[256:]
         psend[:, :, cols] = proj.reshape(NV, 32, width)
         measured = mrecv[:, :, cols].astype(F32).reshape(256, width)
         weighted = rrecv[:, :, cols].astype(F32).reshape(256, width) * (measured - proj)
         part = jnp.dot(atb[...], weighted.astype(BF16), preferred_element_type=F32)
         part = part.astype(BF16)
-        if j == 0:
-            zsend0[...] = part.reshape(NX, 128, width)
+        if j < 2:
+            zsend0[j] = part.reshape(NX, 128, width)
             for o in (2, 1, 3):
-                send(zsend0.at[lax.rem(x + o, NX)], zrecv0.at[o - 1], xp(o), Z0X_S, Z0X_R)
+                send(zsend0.at[j, lax.rem(x + o, NX)], zrecv0.at[j, o - 1], xp(o), Z0X_S, (Z0X_R, Z0XB_R)[j])
         else:
             zsend1[...] = part.reshape(NX, NZ, S, width)
             for o in FAR_Z:
@@ -222,13 +222,14 @@
 
     lax.fori_loop(8, 18, turn, 0)
 
-    arrived(zrecv0, Z0X_R)
-    total = zsend0[x].astype(F32)
-    for o in range(NX - 1):
-        total += zrecv0[o].astype(F32)
-    ssend0[...] = total.astype(BF16).reshape(NZ, S, 256)
-    for o in FAR_Z:
-        send(ssend0.at[lax.rem(z + o, NZ)], srecv0.at[o - 1], zp(o), Z0Z_S, Z0Z_R)
+    for j in range(2):
+        arrived(zrecv0.at[j], (Z0X_R, Z0XB_R)[j])
+        total = zsend0[j, x].astype(F32)
+        for o in range(NX - 1):
+            total += zrecv0[j, o].astype(F32)
+        ssend0[j] = total.astype(BF16).reshape(NZ, S, 128)
+        for o in FAR_Z:
+            send(ssend0.at[j, lax.rem(z + o, NZ)], srecv0.at[j, o - 1], zp(o), Z0Z_S, (Z0Z_R, Z0ZB_R)[j])
 
     arrived(zrecv1, Z1Z_R)
     total = zsend1[:, z].astype(F32)
@@ -240,11 +241,12 @@
 
     lax.fori_loop(18, DC // 128, turn, 0)
 
-    arrived(srecv0, Z0Z_R)
-    total = ssend0[z].astype(F32)
-    for o in range(NZ - 1):
-        total += srecv0[o].astype(F32)
-    sall[g, :, :256] = total.astype(BF16)
+    for j in range(2):
+        arrived(srecv0.at[j], (Z0Z_R, Z0ZB_R)[j])
+        total = ssend0[j, z].astype(F32)
+        for o in range(NZ - 1):
+            total += srecv0[j, o].astype(F32)
+        sall[g, :, j * 128 : (j + 1) * 128] = total.astype(BF16)
 
     arrived(srecv1, Z1X_R)
     total = ssend1[x].astype(F32)
@@ -327,13 +329,13 @@
             pltpu.VMEM((NV, 32, CW), BF16),
             pltpu.VMEM((NV, 32, CW), F32),
             pltpu.VMEM((NV, 32, CW), F32),
-            pltpu.VMEM((NX, 128, 256), BF16),
+            pltpu.VMEM((2, NX, 128, 128), BF16),
             pltpu.VMEM((NX, NZ, S, 128), BF16),
-            pltpu.VMEM((NX - 1, 128, 256), BF16),
+            pltpu.VMEM((2, NX - 1, 128, 128), BF16),
             pltpu.VMEM((NZ - 1, NX, S, 128), BF16),
-            pltpu.VMEM((NZ, S, 256), BF16),
+            pltpu.VMEM((2, NZ, S, 128), BF16),
             pltpu.VMEM((NX, S, 128), BF16),
-            pltpu.VMEM((NZ - 1, S, 256), BF16),
+            pltpu.VMEM((2, NZ - 1, S, 128), BF16),
             pltpu.VMEM((NX - 1, S, 128), BF16),
             pltpu.VMEM((NV, S, CW), BF16),
             pltpu.VMEM((NY, S, KV), F32),

time: 39 us -> 39.6 us (1.015)
  Pallas kernels: 37.5 us -> 38.2 us
    pallas_call x1, Pallas kernels: 36.8 us -> 37.4 us  [body(): pl.pallas_call(kernel, out_shape=(pltpu.VMEM((S, KV), F32), pltpu.VMEM((3...]
where the time goes in v8:
time: 39.6 us; the launch traced here: 39.4 us
  Pallas kernels  38.2 us (96%)
  between operations  1.29 us (3%)
    pallas_call x1, Pallas kernels, body(): pl.pallas_call(kernel, out_shape=(pltpu.VMEM((S, KV), F32), pltpu.VMEM((3...  37.4 us

profile of v8, /device:TPU:1, one launch (start us, length us, event | category | flops | bytes accessed | tf_op | source)
XLA Modules:
  0.0 39.4 jit_solution(8469197711047332623)
XLA Ops:
  1.3 37.4 %sirt.1 = (f32[16,1024]{1,0:T(8,128)S(1)}, f32[32,3072]{1,0:T(8,128)S(1)}) custom-call(f32[16,1024]{1,0:T(8,128)} %vol_hbm.1, f32[8,16,80]{2,1,0:T(8,128)} %bitcast.9, bf16[1024,3072]{1,0:T(8,128)(2,1)} %c_hbm.1, s32[1]{0:T(128)S(6)} %copy.11.tile_hbm, s32[8]{0:T(128)} %offset_hbm.1, s32[8]{0:T(128)} %angle_hbm.1, f32[32,3072]{1,0:T(8,128)} %bitcast.7, ...), custom_call_target="tpu_custom_call" | custom-call | flops 500000000 | bytes 3000000 | tf_op jit(solution)/shard_map/sirt/pallas_call | solution.py:301
  38.7 0.8 %hand_over.1 = (f32[16,1024]{1,0:T(8,128)}, f32[4,8,3072]{2,1,0:T(8,128)}) custom-call(f32[16,1024]{1,0:T(8,128)S(1)} %get-tuple-element.4.upd_in, f32[4,8,3072]{2,1,0:T(8,128)S(1)} %bitcast.6), custom_call_target="tpu_custom_call" | custom-call | tf_op jit(solution)/shard_map/hand_over/pallas_call | solution.py:353
